TPU v7x, 256 devices: a whole 4x4x8 slice. The times are simulated.
256 devices in a mesh: row: 16 (over x, y), col: 16 (over z, core).
Axes of the slice: x: 4, y: 4, z: 8, core: 2. Of those that a mesh axis runs over, the one named last changes fastest.
Arguments:
- tiles: float32 [16, 16, 3, 128, 64, 128], P('row', 'col'), may hold values from -0.0625 to 0.0625
- tile_coords: int32 [16, 16, 3, 2, 256], P('row', 'col'), may hold values from 0 to 31, as said below
- tile_count: int32 [16, 16, 3], P('row', 'col'), may hold values from 32 to 256, as said below
- seeds: int32 [128], replicated, may hold values from 0 to 32767
- chain: int32 [3], replicated, may hold values from 0 to 2
Outputs:
- answers: float32 [32768, 128], P(('row', 'col'))
Inputs may be any that keep to these rules, and one draw needn't show every extreme that they name: tile_coords[..., 0, :] is below 16 * 2 and tile_coords[..., 1, :] below 16 * 2; pairs may repeat. `tile_count`: each count is 256 divided by 1, 2, 4 or 8; for every relation some device has all 256 slots live.
All inputs are finite; a program needn't handle non-finite values.
Results may differ from a plain program's by a relative error of at most 0.0003.
Values sent between devices are 32-bit elements; how exact they have to be, the bound alone decides.
A program may use at most 128 MiB of HBM per device.

v0:
```python
import jax
import jax.numpy as jnp
from jax import lax
from jax.sharding import PartitionSpec as P

QUERIES = 128
TILE = 64
BLOCKS_DEV = 2
HOPS = 3


def paired_products(pair_values, picked):
    pair_total = pair_values.shape[0]
    split_values = pair_values.reshape(pair_total, TILE, 2, TILE)
    split_states = picked.reshape(pair_total, 2, TILE, QUERIES)
    product = jnp.einsum(
        "sahb,shbq->shaq", split_values, split_states, precision=lax.Precision.HIGHEST
    )
    return product.reshape(pair_total * 2, TILE, QUERIES)


def collect_rows(product, targets, live, out_blocks):
    slot_total = targets.shape[0]
    block_ids = jnp.arange(out_blocks, dtype=jnp.int32)
    selector = ((targets[None, :] == block_ids[:, None]) & live[None, :]).astype(jnp.float32)
    flat = product.reshape(slot_total, -1)
    return jnp.dot(
        selector, flat, precision=lax.Precision.HIGHEST, preferred_element_type=jnp.float32
    )


def local_products(column_states, values, coords, live_count, out_blocks):
    blocks = column_states.reshape(-1, TILE, QUERIES)
    slot_total = coords.shape[1]
    picked = blocks[coords[1]]
    product = paired_products(values, picked)
    live = jnp.arange(slot_total, dtype=jnp.int32) < live_count
    summed = collect_rows(product, coords[0], live, out_blocks)
    return summed.reshape(out_blocks * TILE, QUERIES)


def shards(tiles, tile_coords, tile_count, seeds, chain):
    row_total = lax.axis_size("row")
    col_total = lax.axis_size("col")
    my_row = lax.axis_index("row")
    my_col = lax.axis_index("col")
    rows_here = BLOCKS_DEV * TILE
    out_blocks = col_total * BLOCKS_DEV
    all_values = tiles[0, 0]
    all_coords = tile_coords[0, 0]
    all_counts = tile_count[0, 0]
    offsets = jnp.arange(rows_here, dtype=jnp.int32)
    entity_ids = (my_row * col_total + my_col) * rows_here + offsets
    seed_states = (entity_ids[:, None] == seeds[None, :]).astype(jnp.float32)
    column_states = lax.all_gather(seed_states, "row", axis=0, tiled=True)
    for step_index in range(HOPS):
        relation = chain[step_index]
        values = lax.dynamic_index_in_dim(all_values, relation, 0, keepdims=False)
        coords = lax.dynamic_index_in_dim(all_coords, relation, 0, keepdims=False)
        live_count = lax.dynamic_index_in_dim(all_counts, relation, 0, keepdims=False)
        partial_value = local_products(column_states, values, coords, live_count, out_blocks)
        owned = lax.psum_scatter(partial_value, "col", scatter_dimension=0, tiled=True)
        if step_index + 1 < HOPS:
            column_states = lax.all_gather(owned, "row", axis=0, tiled=True)
    squares = jnp.sum(owned * owned, axis=0)
    totals = lax.psum(squares, ("row", "col"))
    entity_total = row_total * col_total * rows_here
    return owned * lax.rsqrt(totals / entity_total + 1e-06)


def solution(mesh):
    in_specs = (
        P("row", "col", None, None, None, None),
        P("row", "col", None, None, None),
        P("row", "col", None),
        P(),
        P(),
    )
    out_specs = P(("row", "col"), None)
    return jax.shard_map(shards, mesh=mesh, in_specs=in_specs, out_specs=out_specs, check_vma=False)
```

profile of v0, /device:TPU:1, one launch (start us, length us, event | category | flops | bytes accessed | tf_op | source)
XLA Modules:
  0.0 496.6 jit_solution(6926458707416233631)
XLA Ops:
  6.5 0.0 all-gather.4.cloned.1.call-start
  6.5 1.4 compare_convert_fusion
  7.9 0.0 all-gather.4.cloned.1.call-update
  7.9 0.0 reduce-scatter.4.cloned.1.call-start
  8.0 1.4 fusion.24
  15.1 10.1 %constant_dynamic-slice_fusion.3 = (f32[1,1,1,128,64,128]{5,4,3,2,1,0:T(8,128)}, f32[1,1,1,128,64,128]{5,4,3,2,1,0:T(8,128)}, f32[1,1,1,128,64,128]{5,4,3,2,1,0:T(8,128)}) fusion(f32[1,1,3,128,64,128]{5,4,3,2,1,0:T(8,128)} %param.5, s32[]{:T(128)S(6)} %select_n.50, s32[]{:T(128)S(6)} %select_n.49, s32[]{:T(128)S(6)} %select_n.48), kind=kLoop, calls=%fused_computation.36 | loop fusion | bytes 25165836 | tf_op jit(solution)/shard_map/jit(dynamic_index_in_dim)/dynamic_slice | solution.py:58
  25.2 5.5 %copy.14 = f32[1,1,1,128,64,128]{3,5,4,2,1,0:T(8,128)} copy(f32[1,1,1,128,64,128]{5,4,3,2,1,0:T(8,128)} %get-tuple-element.5) | data formatting | bytes 8388608
  30.7 0.0 copy-start.1
  30.7 0.0 copy-start
  30.7 9.2 %copy.9 = f32[128,64,2,64]{3,1,2,0:T(8,128)} copy(f32[128,64,2,64]{0,3,2,1:T(8,128)} %bitcast.63) | data formatting | bytes 8388608 | tf_op jit(solution)/shard_map/reshape | solution.py:14
  39.9 0.0 copy-done.1
  39.9 0.6 constant_dynamic-slice_fusion.10
  40.5 0.6 iota_compare_fusion.3
  41.1 0.0 copy-done
  41.2 18.7 %all-gather.4.cloned.1.call-done = f32[2048,128]{1,0:T(8,128)} async-done(((f32[128,128]{1,0:T(8,128)}), f32[2048,128]{1,0:T(8,128)}) %all-gather.4.cloned.1.call-update) | async-done | bytes 1048592 | tf_op jit(solution)/shard_map/all_gather | solution.py:55
  59.9 5.6 %gather_fusion = f32[256,64,128]{2,1,0:T(8,128)} fusion(f32[32,64,128]{2,1,0:T(8,128)} %bitcast.54, s32[1024]{0:T(1024)S(1)} %pad_clamp_fusion.2), kind=kCustom, calls=%fused_computation | custom fusion | bytes 16778240 | tf_op jit(solution)/shard_map/gather | solution.py:35
  65.5 12.5 %fusion.25 = f32[128,2,64,128]{3,2,1,0:T(8,128)S(1)} fusion(f32[128,64,2,64]{3,1,2,0:T(8,128)} %copy.9, f32[128,2,64,128]{3,2,1,0:T(8,128)} %bitcast.60), kind=kOutput, calls=%fused_computation.54 | convolution fusion | flops 1610612736 | bytes 20971520 | tf_op jit(solution)/shard_map/sahb,shbq->shaq/dot_general | solution.py:16
  78.0 7.7 %fusion.6 = f32[32,8192]{1,0:T(8,128)S(1)} fusion(f32[32,8,64,128]{3,2,1,0:T(8,128)S(1)} %bitcast.58, s32[256]{0:T(256)S(1)} %bitcast.68, pred[256]{0:T(512)(128)(4,1)S(1)} %iota_compare_fusion.3), kind=kOutput, calls=%fused_computation.9 | convolution fusion | flops 805322752 | bytes 9438464 | tf_op jit(solution)/shard_map/dot_general | solution.py:27
  85.8 1.1 reshape.176
  86.9 0.0 reduce-scatter.4.cloned.1.call-update
  86.9 0.0 all-gather.6.cloned.1.call-start
  87.0 55.2 %reduce-scatter.4.cloned.1.call-done = f32[128,128]{1,0:T(8,128)} async-done(((f32[2048,128]{1,0:T(8,128)}), f32[128,128]{1,0:T(8,128)}) %reduce-scatter.4.cloned.1.call-update) | async-done | bytes 65552 | tf_op jit(solution)/shard_map/reduce_scatter | solution.py:62
  142.1 0.0 all-gather.6.cloned.1.call-update
  142.2 0.0 reduce-scatter.6.cloned.1.call-start
  142.2 6.0 %copy.13 = f32[1,1,1,128,64,128]{3,5,4,2,1,0:T(8,128)} copy(f32[1,1,1,128,64,128]{5,4,3,2,1,0:T(8,128)} %get-tuple-element.6) | data formatting | bytes 8388608
  148.2 9.2 %copy.10 = f32[128,64,2,64]{3,1,2,0:T(8,128)} copy(f32[128,64,2,64]{0,3,2,1:T(8,128)} %bitcast.64) | data formatting | bytes 8388608 | tf_op jit(solution)/shard_map/reshape | solution.py:14
  157.4 0.6 iota_compare_fusion.4
  158.0 34.6 %all-gather.6.cloned.1.call-done = f32[2048,128]{1,0:T(8,128)} async-done(((f32[128,128]{1,0:T(8,128)}), f32[2048,128]{1,0:T(8,128)}) %all-gather.6.cloned.1.call-update) | async-done | bytes 1048592 | tf_op jit(solution)/shard_map/all_gather | solution.py:64
  192.6 5.6 %gather_fusion.1 = f32[256,64,128]{2,1,0:T(8,128)} fusion(f32[32,64,128]{2,1,0:T(8,128)} %bitcast.56, s32[1024]{0:T(1024)S(1)} %pad_clamp_fusion.1), kind=kCustom, calls=%fused_computation.1 | custom fusion | bytes 16778240 | tf_op jit(solution)/shard_map/gather | solution.py:35
  198.2 12.4 %fusion.26 = f32[128,2,64,128]{3,2,1,0:T(8,128)S(1)} fusion(f32[128,64,2,64]{3,1,2,0:T(8,128)} %copy.10, f32[128,2,64,128]{3,2,1,0:T(8,128)} %bitcast.61), kind=kOutput, calls=%fused_computation.55 | convolution fusion | flops 1610612736 | bytes 20971520 | tf_op jit(solution)/shard_map/sahb,shbq->shaq/dot_general | solution.py:16
  210.6 7.7 %fusion.3 = f32[32,8192]{1,0:T(8,128)S(1)} fusion(f32[32,8,64,128]{3,2,1,0:T(8,128)S(1)} %bitcast.59, s32[256]{0:T(256)S(1)} %bitcast.67, pred[256]{0:T(512)(128)(4,1)S(1)} %iota_compare_fusion.4), kind=kOutput, calls=%fused_computation.6 | convolution fusion | flops 805322752 | bytes 9438464 | tf_op jit(solution)/shard_map/dot_general | solution.py:27
  218.3 1.1 reshape.179
  219.5 0.0 reduce-scatter.6.cloned.1.call-update
  219.5 0.0 all-gather.8.cloned.1.call-start
  219.6 55.2 %reduce-scatter.6.cloned.1.call-done = f32[128,128]{1,0:T(8,128)} async-done(((f32[2048,128]{1,0:T(8,128)}), f32[128,128]{1,0:T(8,128)}) %reduce-scatter.6.cloned.1.call-update) | async-done | bytes 65552 | tf_op jit(solution)/shard_map/reduce_scatter | solution.py:62
  274.8 0.0 all-gather.8.cloned.1.call-update
  274.8 0.0 reduce-scatter.8.cloned.1.call-start
  274.8 5.7 %copy.12 = f32[1,1,1,128,64,128]{3,5,4,2,1,0:T(8,128)} copy(f32[1,1,1,128,64,128]{5,4,3,2,1,0:T(8,128)} %get-tuple-element.7) | data formatting | bytes 8388608
  280.5 9.2 %copy.11 = f32[128,64,2,64]{3,1,2,0:T(8,128)} copy(f32[128,64,2,64]{0,3,2,1:T(8,128)} %bitcast.65) | data formatting | bytes 8388608 | tf_op jit(solution)/shard_map/reshape | solution.py:14
  289.7 0.6 iota_compare_fusion.5
  290.3 34.6 %all-gather.8.cloned.1.call-done = f32[2048,128]{1,0:T(8,128)} async-done(((f32[128,128]{1,0:T(8,128)}), f32[2048,128]{1,0:T(8,128)}) %all-gather.8.cloned.1.call-update) | async-done | bytes 1048592 | tf_op jit(solution)/shard_map/all_gather | solution.py:64
  324.9 5.6 %gather_fusion.2 = f32[256,64,128]{2,1,0:T(8,128)} fusion(f32[32,64,128]{2,1,0:T(8,128)} %bitcast.55, s32[1024]{0:T(1024)S(1)} %pad_clamp_fusion), kind=kCustom, calls=%fused_computation.2 | custom fusion | bytes 16778240 | tf_op jit(solution)/shard_map/gather | solution.py:35
  330.5 12.5 %fusion.27 = f32[128,2,64,128]{3,2,1,0:T(8,128)S(1)} fusion(f32[128,64,2,64]{3,1,2,0:T(8,128)} %copy.11, f32[128,2,64,128]{3,2,1,0:T(8,128)} %bitcast.62), kind=kOutput, calls=%fused_computation.56 | convolution fusion | flops 1610612736 | bytes 20971520 | tf_op jit(solution)/shard_map/sahb,shbq->shaq/dot_general | solution.py:16
  343.0 7.7 %fusion = f32[32,8192]{1,0:T(8,128)S(1)} fusion(f32[32,8,64,128]{3,2,1,0:T(8,128)S(1)} %bitcast.57, s32[256]{0:T(256)S(1)} %bitcast.66, pred[256]{0:T(512)(128)(4,1)S(1)} %iota_compare_fusion.5), kind=kOutput, calls=%fused_computation.3 | convolution fusion | flops 805322752 | bytes 9438464 | tf_op jit(solution)/shard_map/dot_general | solution.py:27
  350.7 1.1 reshape.182
  351.9 0.0 reduce-scatter.8.cloned.1.call-update
  351.9 55.2 %reduce-scatter.8.cloned.1.call-done = f32[128,128]{1,0:T(8,128)} async-done(((f32[2048,128]{1,0:T(8,128)}), f32[128,128]{1,0:T(8,128)}) %reduce-scatter.8.cloned.1.call-update) | async-done | bytes 65552 | tf_op jit(solution)/shard_map/reduce_scatter | solution.py:62
  407.1 0.9 multiply_reduce_fusion
  408.0 80.0 %psum.7 = f32[128]{0:T(128)S(1)} all-reduce(f32[128]{0:T(128)S(1)} %multiply_reduce_fusion), channel_id=1, replica_groups=mesh['row'=16,'col'=16] {'row','col'}, use_global_device_ids=true, to_apply=%region_4.5 | all-reduce | flops 128 | bytes 1024 | tf_op jit(solution)/shard_map/psum | solution.py:66
  488.0 1.5 broadcast_multiply_fusion
  (7 shorter events, 0.1 us)
Async XLA Ops:
  6.5 53.4 %all-gather.4.cloned.1.call-start = ((), (), s32[]{:S(2)}) async-start(), calls=%async_computation.3 | async-start | bytes 1114112 | tf_op jit(solution)/shard_map/all_gather | solution.py:55
  7.9 134.2 %reduce-scatter.4.cloned.1.call-start = ((), (), s32[]{:S(2)}) async-start(), calls=%async_computation.4 | async-start | bytes 1114112 | tf_op jit(solution)/shard_map/reduce_scatter | solution.py:62
  30.7 9.2 %copy-start.1 = (s32[1,1,3]{2,1,0:T(1,128)S(1)}, s32[1,1,3]{2,1,0:T(1,128)}, u32[]{:S(2)}) copy-start(s32[1,1,3]{2,1,0:T(1,128)} %param.7) | copy-start | bytes 40
  30.7 10.5 %copy-start = (s32[1,1,3,2,256]{4,3,2,1,0:T(2,128)S(1)}, s32[1,1,3,2,256]{4,3,2,1,0:T(2,128)}, u32[]{:S(2)}) copy-start(s32[1,1,3,2,256]{4,3,2,1,0:T(2,128)} %param.6) | copy-start | bytes 18436
  86.9 105.7 %all-gather.6.cloned.1.call-start = ((), (), s32[]{:S(2)}) async-start(), calls=%async_computation.5 | async-start | bytes 1114112 | tf_op jit(solution)/shard_map/all_gather | solution.py:64
  142.2 132.6 %reduce-scatter.6.cloned.1.call-start = ((), (), s32[]{:S(2)}) async-start(), calls=%async_computation.6 | async-start | bytes 1114112 | tf_op jit(solution)/shard_map/reduce_scatter | solution.py:62
  219.5 105.4 %all-gather.8.cloned.1.call-start = ((), (), s32[]{:S(2)}) async-start(), calls=%async_computation.7 | async-start | bytes 1114112 | tf_op jit(solution)/shard_map/all_gather | solution.py:64
  274.8 132.3 %reduce-scatter.8.cloned.1.call-start = ((), (), s32[]{:S(2)}) async-start(), calls=%async_computation.8 | async-start | bytes 1114112 | tf_op jit(solution)/shard_map/reduce_scatter | solution.py:62
Sparse Core Ops, SparseCore 0:
  9.8 50.0 all-gather.3
  87.0 55.0 reduce-scatter.3
  144.9 47.6 all-gather.5
  219.6 55.0 reduce-scatter.5
  277.0 47.8 all-gather.7
  352.0 55.0 reduce-scatter.7
where the time goes:
time: 503 us; the launch traced here: 497 us
  waiting for transfers between devices  254 us (50%)
  blocking collectives  80 us (16%)
  local copies, waits for them, and re-layouts  76.9 us (15%)
  matrix products  60.7 us (12%)
  between operations  19.5 us (4%)
  other arithmetic  5.64 us (1%)
    reduce_scatter x3, waiting for transfers between devices, shards(): lax.psum_scatter(partial_value, 'col', scatter_dimension=0, tiled=True)  166 us
    psum x1, blocking collectives, shards(): totals = lax.psum(squares, ('row', 'col'))  80 us
    all_gather x2, waiting for transfers between devices, shards(): column_states = lax.all_gather(owned, 'row', axis=0, tiled=True)  69.2 us
    dot_general x3, matrix products, paired_products(): jnp.einsum('sahb,shbq->shaq', split_values, split_states, precision=lax.P...  37.5 us
    reshape x3, local copies, waits for them, and re-layouts, paired_products(): split_values = pair_values.reshape(pair_total, TILE, 2, TILE)  27.5 us
    dot_general x3, matrix products, collect_rows(): jnp.dot(selector, flat, precision=lax.Precision.HIGHEST, preferred_elemen...  23.2 us
    all_gather x1, waiting for transfers between devices, shards(): column_states = lax.all_gather(seed_states, 'row', axis=0, tiled=True)  18.7 us
    unnamed x7, local copies, waits for them, and re-layouts  17.1 us
  transfers between devices with their start and end apart: 6, of which 6 were waited for; matrix products, arithmetic and copies ran while one was open for 12% of the time, Pallas kernels for 0%

commit v1 on v0

v1 whole, which is shorter than its diff:
```python
import functools

import jax
import jax.numpy as jnp
from jax import lax
from jax.experimental import pallas as pl
from jax.experimental.pallas import tpu as pltpu
from jax.sharding import PartitionSpec as P

QUERIES = 128
TILE = 64
BLOCK = 128
SLOTS = 256
RELATIONS = 3
HOPS = 3
NX, NY, NZ = 4, 4, 8
NROW = NX * NY
NCOL = NZ * 2
CELLS = 2 * NCOL * NROW
ENTITIES = NROW * NCOL * BLOCK
MESH = pl.DeviceIdType.MESH
F32 = jnp.float32
BF16 = jnp.bfloat16


def merge_kernel(chain, count, coords, tiles, cells, table, slots, merged, in_sem, out_sem):
    loads = []
    for h in range(HOPS):
        copy = pltpu.make_async_copy(tiles.at[chain[h]], slots.at[h], in_sem.at[h])
        copy.start()
        loads.append(copy)
    high = lax.broadcasted_iota(jnp.int32, (TILE, 2 * TILE), 1) >= TILE
    stores = []
    for h in range(HOPS):
        m = chain[h]

        @pl.loop(0, CELLS // 16)
        def _(n):
            for k in range(16):
                table[h * CELLS + n * 16 + k] = SLOTS

        merged[h, SLOTS] = jnp.zeros((TILE, 2 * TILE), F32)
        loads[h].wait()

        @pl.loop(0, count[m] // 4)
        def _(n):
            for k in range(4):
                t = n * 4 + k
                i = coords[m, 0, t]
                j = coords[m, 1, t]
                block = ((i // 2) % 2) * 16 + (i // 4) * 2 + i % 2
                key = h * CELLS + block * NROW + j // 2
                side = j % 2
                found = table[key]
                fresh = found == SLOTS
                target = jnp.where(fresh, t, found)
                table[key] = target
                shift = jnp.where(side == k % 2, 0, TILE)
                value = pltpu.roll(slots[h, n * 2 + k // 2], shift, 1)
                value = jnp.where(high == (side == 1), value, 0.0)
                merged[h, target] = value + jnp.where(fresh, 0.0, merged[h, target])

        copy = pltpu.make_async_copy(merged.at[h], cells.at[h], out_sem.at[h])
        copy.start()
        stores.append(copy)
    for copy in stores:
        copy.wait()


def merge(chain, count, coords, tiles):
    smem = pl.BlockSpec(memory_space=pltpu.SMEM)
    anywhere = pl.BlockSpec(memory_space=pl.ANY)
    return pl.pallas_call(
        merge_kernel,
        out_shape=(
            jax.ShapeDtypeStruct((HOPS, SLOTS + 1, TILE, 2 * TILE), F32),
            jax.ShapeDtypeStruct((HOPS * CELLS,), jnp.int32),
        ),
        in_specs=[smem, smem, smem, anywhere],
        out_specs=(anywhere, smem),
        scratch_shapes=[
            pltpu.VMEM((HOPS, SLOTS // 2, TILE, 2 * TILE), F32),
            pltpu.VMEM((HOPS, SLOTS + 1, TILE, 2 * TILE), F32),
            pltpu.SemaphoreType.DMA((HOPS,)),
            pltpu.SemaphoreType.DMA((HOPS,)),
        ],
        compiler_params=pltpu.CompilerParams(vmem_limit_bytes=56 * 2**20),
        name="merge_slots",
    )(chain, count, coords, tiles)


def chain_kernel(
    table, seeds, cells, out,
    held_a, held_b, dense_hi, dense_lo, right, part, cross, ring, state, col_tot, row_tot,
    load_sem, cross_sem, ring_sem, gather_sem, tot_sem,
):
    p = lax.axis_index("row")
    q = lax.axis_index("col")
    x, y = p // NY, p % NY
    z, core = q // 2, q % 2
    other = 1 - core

    def remote(src, dst, send, recv, device):
        return pltpu.make_async_remote_copy(
            src_ref=src, dst_ref=dst, send_sem=send, recv_sem=recv, device_id=device, device_id_type=MESH
        )

    held = (held_a, held_b, held_a)

    def load(h):
        return pltpu.make_async_copy(cells.at[h], held[h], load_sem.at[h])

    load(0).start()
    load(1).start()
    barrier = pltpu.get_barrier_semaphore()

    @pl.loop(1, 16)
    def _(d):
        pl.semaphore_signal(barrier, inc=1, device_id=(p, (q + d) % NCOL), device_id_type=MESH)
        pl.semaphore_signal(barrier, inc=1, device_id=((p + d) % NROW, q), device_id_type=MESH)

    def assemble(h, start, stop):
        @pl.loop(start, stop)
        def _(block):
            rows = pl.ds(pl.multiple_of(block * TILE, TILE), TILE)
            for s in range(NROW):
                value = held[h][table[h * CELLS + block * NROW + s]]
                top = value.astype(BF16)
                dense_hi[s, rows, :] = top
                dense_lo[s, rows, :] = (value - top.astype(F32)).astype(BF16)

    def multiply(half):
        @pl.loop(0, 2)
        def _(m):
            first = half * 8 + m * 4
            rows = pl.ds(pl.multiple_of(first * BLOCK, 4 * BLOCK), 4 * BLOCK)
            left = jnp.concatenate([dense_hi[s, rows, :] for s in range(NROW)], axis=1)
            both = jnp.dot(left, right[...], preferred_element_type=F32)
            left = jnp.concatenate([dense_lo[s, rows, :] for s in range(NROW)], axis=1)
            low = jnp.dot(left, right[:, :QUERIES], preferred_element_type=F32)
            total = both[:, :QUERIES] + both[:, QUERIES:] + low
            part[pl.ds(first, 4)] = total.reshape(4, BLOCK, QUERIES)

    load(0).wait()
    assemble(0, 0, 32)
    load(2).start()
    offsets = lax.broadcasted_iota(jnp.int32, (BLOCK, QUERIES), 0)
    for s in range(NROW):
        ids = (s * NCOL + q) * BLOCK + offsets
        hit = jnp.where(ids == seeds[...], 1.0, 0.0).astype(BF16)
        right[s * BLOCK:(s + 1) * BLOCK, :QUERIES] = hit
        right[s * BLOCK:(s + 1) * BLOCK, QUERIES:] = jnp.zeros((BLOCK, QUERIES), BF16)

    for h in range(HOPS):
        sends = []
        multiply(other)
        if h == 0:
            pl.semaphore_wait(barrier, 30)

        def crossing(o):
            block = (z + o) % NZ
            return remote(
                part.at[other * 8 + block], cross.at[h, block],
                cross_sem.at[0, h, o], cross_sem.at[1, h, o], (p, z * 2 + other),
            )

        order = (4, 3, 5, 2, 6, 1, 7, 0)
        for o in order:
            copy = crossing(o)
            copy.start()
            sends.append(copy)
        multiply(core)

        def half_rows(u):
            return pl.ds(u * TILE, TILE)

        def along(way, k, u, src):
            near = (z + (1 if way == 0 else NZ - 1)) % NZ
            return remote(
                src, ring.at[h, way, k - 1, half_rows(u)],
                ring_sem.at[0, h, way, k - 1, u], ring_sem.at[1, h, way, k - 1, u], (p, near * 2 + core),
            )

        def mine(o):
            return core * 8 + (z + o) % NZ

        def start(way, k, u, src):
            copy = along(way, k, u, src)
            copy.start()
            sends.append(copy)

        for o in order:
            crossing(o).wait_recv()
            part[mine(o)] = part[mine(o)] + cross[h, (z + o) % NZ]
            if o == 4:
                start(0, 4, 0, part.at[mine(4), half_rows(0)])
                start(1, 4, 1, part.at[mine(4), half_rows(1)])
            if o == 3:
                start(0, 3, 1, part.at[mine(3), half_rows(1)])
            if o == 5:
                start(1, 3, 0, part.at[mine(5), half_rows(0)])

        def relay(way, k, u):
            slot = ring.at[h, way, k - 1, half_rows(u)]
            along(way, k, u, slot).wait_recv()
            o = k - 1 if way == 0 else NZ - (k - 1)
            slot[...] = slot[...] + part[mine(o), half_rows(u), :]
            start(way, k - 1, u, slot)

        pieces = iter(range(0, 32, 8))

        def fill():
            if h + 1 < HOPS:
                at = next(pieces)
                if at == 0:
                    load(h + 1).wait()
                assemble(h + 1, at, at + 8)

        fill()
        relay(0, 4, 0)
        relay(1, 4, 1)
        relay(0, 3, 1)
        relay(1, 3, 0)
        fill()
        relay(0, 3, 0)
        relay(1, 3, 1)
        relay(0, 2, 1)
        relay(1, 2, 0)
        fill()
        relay(0, 2, 0)
        relay(1, 2, 1)

        def finished(u):
            for way in range(2):
                along(way, 1, u, ring.at[h, way, 0, half_rows(u)]).wait_recv()
            return part[mine(0), half_rows(u), :] + ring[h, 0, 0, half_rows(u), :] + ring[h, 1, 0, half_rows(u), :]

        if h + 1 < HOPS:
            used = [0, 0]

            def spread(u, source, device):
                copy = remote(
                    state.at[h, source, half_rows(u)], state.at[h, source, half_rows(u)],
                    gather_sem.at[0, h, u, used[u]], gather_sem.at[1, h, u, source], device,
                )
                used[u] += 1
                copy.start()
                sends.append(copy)

            def across(u, d):
                return ((x + d) % NX) * NY + y if u == 0 else x * NY + (y + d) % NY

            def arrived(u, source):
                remote(
                    state.at[h, source, half_rows(u)], state.at[h, source, half_rows(u)],
                    gather_sem.at[0, h, u, 0], gather_sem.at[1, h, u, source], (p, z * 2 + other),
                ).wait_recv()

            for u in range(2):
                state[h, p, half_rows(u), :] = finished(u)
                for d in (2, 1, 3):
                    spread(u, p, (across(u, d), q))
                for d in (2, 1, 3):
                    spread(u, p, (across(1 - u, d), q))
            fill()
            for d in (1, 3, 2):
                for u in range(2):
                    source = across(u, d)
                    arrived(u, source)
                    for e in (2, 1, 3):
                        spot = (x * NY + (y + e) % NY if u == 0 else ((x + e) % NX) * NY + y, q)
                        spread(u, source, spot)
            for u in range(2):
                for d in range(NX):
                    for e in (1, 2, 3):
                        if u == 0:
                            arrived(u, ((x + d) % NX) * NY + (y + e) % NY)
                        else:
                            arrived(u, ((x + e) % NX) * NY + (y + d) % NY)
            for s in range(NROW):
                value = state[h, s]
                top = value.astype(BF16)
                right[s * BLOCK:(s + 1) * BLOCK, :QUERIES] = top
                right[s * BLOCK:(s + 1) * BLOCK, QUERIES:] = (value - top.astype(F32)).astype(BF16)
        else:
            for u in range(2):
                out[half_rows(u), :] = finished(u)
        for copy in sends:
            copy.wait_send()

    owned = out[...]
    col_tot[q] = jnp.sum((owned * owned).reshape(16, 8, QUERIES), axis=0)

    def total(d, stage):
        if stage == 0:
            return remote(col_tot.at[q], col_tot.at[q], tot_sem.at[0, 0, d], tot_sem.at[1, 0, d], (p, (q + d) % NCOL))
        return remote(row_tot.at[p], row_tot.at[p], tot_sem.at[0, 1, d], tot_sem.at[1, 1, d], ((p + d) % NROW, q))

    for stage in range(2):
        @pl.loop(1, 16)
        def _(d):
            total(d, stage).start()

        @pl.loop(1, 16)
        def _(d):
            total(d, stage).wait()

        if stage == 0:
            row_tot[p] = jnp.sum(col_tot[...], axis=0)
    totals = jnp.sum(jnp.sum(row_tot[...], axis=0), axis=0, keepdims=True)
    out[...] = owned * lax.rsqrt(totals / ENTITIES + 1e-06)


def run_chain(table, seeds, cells):
    smem = pl.BlockSpec(memory_space=pltpu.SMEM)
    vmem = pl.BlockSpec(memory_space=pltpu.VMEM)
    anywhere = pl.BlockSpec(memory_space=pl.ANY)
    return pl.pallas_call(
        chain_kernel,
        out_shape=jax.ShapeDtypeStruct((BLOCK, QUERIES), F32),
        in_specs=[smem, vmem, anywhere],
        out_specs=vmem,
        scratch_shapes=[
            pltpu.VMEM((SLOTS + 1, TILE, 2 * TILE), F32),
            pltpu.VMEM((SLOTS + 1, TILE, 2 * TILE), F32),
            pltpu.VMEM((NROW, NCOL * BLOCK, BLOCK), BF16),
            pltpu.VMEM((NROW, NCOL * BLOCK, BLOCK), BF16),
            pltpu.VMEM((NROW * BLOCK, 2 * QUERIES), BF16),
            pltpu.VMEM((NCOL, BLOCK, QUERIES), F32),
            pltpu.VMEM((HOPS, NZ, BLOCK, QUERIES), F32),
            pltpu.VMEM((HOPS, 2, 4, BLOCK, QUERIES), F32),
            pltpu.VMEM((HOPS - 1, NROW, BLOCK, QUERIES), F32),
            pltpu.VMEM((NCOL, 8, QUERIES), F32),
            pltpu.VMEM((NROW, 8, QUERIES), F32),
            pltpu.SemaphoreType.DMA((HOPS,)),
            pltpu.SemaphoreType.DMA((2, HOPS, NZ)),
            pltpu.SemaphoreType.DMA((2, HOPS, 2, 4, 2)),
            pltpu.SemaphoreType.DMA((2, HOPS - 1, 2, 16)),
            pltpu.SemaphoreType.DMA((2, 2, 16)),
        ],
        compiler_params=pltpu.CompilerParams(
            collective_id=0, has_side_effects=True, vmem_limit_bytes=56 * 2**20
        ),
        name="relation_chain",
    )(table, seeds, cells)


def shards(tiles, tile_coords, tile_count, seeds, chain):
    cells, table = merge(chain, tile_count[0, 0], tile_coords[0, 0], tiles[0, 0])
    return run_chain(table, seeds.reshape(1, QUERIES), cells)


def solution(mesh):
    in_specs = (
        P("row", "col", None, None, None, None),
        P("row", "col", None, None, None),
        P("row", "col", None),
        P(),
        P(),
    )
    out_specs = P(("row", "col"), None)
    return jax.shard_map(shards, mesh=mesh, in_specs=in_specs, out_specs=out_specs, check_vma=False)
```

time: 503 us -> 135 us (0.27); the launches traced: 497 us -> 135 us
  waiting for transfers between devices: 254 us -> 0 us
  Pallas kernels: 0 us -> 134 us
  blocking collectives: 80 us -> 0 us
  local copies, waits for them, and re-layouts: 76.9 us -> 1.47 us
  matrix products: 60.7 us -> 0 us
  between operations: 19.5 us -> 0.02 us
  other arithmetic: 5.64 us -> 0 us
    reduce_scatter x3 -> x0, waiting for transfers between devices: 166 us -> none  [shards(): lax.psum_scatter(partial_value, 'col', scatter_dimension=0, tiled=True)]
    pallas_call x0 -> x2, Pallas kernels: none -> 134 us  [the longest x1 114 us: run_chain(): pl.pallas_call(chain_kernel, out_shape=jax.ShapeDtypeStruct((BLOCK, QUERI...]
    all_gather x3 -> x0, waiting for transfers between devices: 87.9 us -> none  [the longest x2 69.2 us: shards(): column_states = lax.all_gather(owned, 'row', axis=0, tiled=True)]
    psum x1 -> x0, blocking collectives: 80 us -> none  [shards(): totals = lax.psum(squares, ('row', 'col'))]
    dot_general x6 -> x0, matrix products: 60.7 us -> none  [the longest x3 37.5 us: paired_products(): jnp.einsum('sahb,shbq->shaq', split_values, split_states, precision=lax.P...]
    reshape x6 -> x0, local copies, waits for them, and re-layouts: 30.9 us -> none  [the longest x3 27.5 us: paired_products(): split_values = pair_values.reshape(pair_total, TILE, 2, TILE)]
    gather x3 -> x0, local copies, waits for them, and re-layouts: 16.7 us -> none  [local_products(): picked = blocks[coords[1]]]
    unnamed x7 -> x1, local copies, waits for them, and re-layouts: 17.1 us -> 1.47 us
  transfers between devices with their start and end apart: 6 -> 0, of which waited for: 6 -> 0; matrix products, arithmetic and copies ran while one was open for 12% -> 0% of each run, Pallas kernels for 0% -> 0%
where the time goes in v1:
time: 135 us
  Pallas kernels  134 us (99%)
  local copies, waits for them, and re-layouts  1.47 us (1%)
    pallas_call x1, Pallas kernels, run_chain(): pl.pallas_call(chain_kernel, out_shape=jax.ShapeDtypeStruct((BLOCK, QUERI...  114 us
    pallas_call x1, Pallas kernels, merge(): pl.pallas_call(merge_kernel, out_shape=(jax.ShapeDtypeStruct((HOPS, SLOTS...  19.4 us

profile of v1, /device:TPU:1, one launch (start us, length us, event | category | flops | bytes accessed | tf_op | source)
XLA Modules:
  0.0 135.3 jit_solution(11199664175739721388)
XLA Ops:
  0.0 19.4 %merge_slots.1 = (f32[3,257,64,128]{3,2,1,0:T(8,128)}, s32[1536]{0:T(1024)}) custom-call(s32[3]{0:T(128)} %chain.1, s32[3]{0:T(128)} %bitcast.7, s32[3,2,256]{2,1,0:T(2,128)} %bitcast.5, f32[3,128,64,128]{3,2,1,0:T(8,128)} %bitcast.4), custom_call_target="tpu_custom_call" | custom-call | tf_op jit(solution)/shard_map/merge_slots/pallas_call | solution.py:73
  19.4 114.4 %relation_chain.1 = f32[128,128]{1,0:T(8,128)} custom-call(s32[1536]{0:T(1024)} %get-tuple-element.7.table, s32[1,128]{1,0:T(1,128)} %bitcast.6, f32[3,257,64,128]{3,2,1,0:T(8,128)} %get-tuple-element.8.cells), custom_call_target="tpu_custom_call" | custom-call | tf_op jit(solution)/shard_map/relation_chain/pallas_call | solution.py:318
  133.8 1.5 %copy.7 = f32[128,128]{1,0:T(8,128)} copy(f32[128,128]{1,0:T(8,128)} %relation_chain.1) | data formatting | bytes 131072

commit v2 on v1

v2 whole, which is shorter than its diff:
```python
import jax
import jax.numpy as jnp
from jax import lax
from jax.experimental import pallas as pl
from jax.experimental.pallas import tpu as pltpu
from jax.sharding import PartitionSpec as P

QUERIES = 128
TILE = 64
BLOCK = 128
SLOTS = 256
HOPS = 3
NX, NY, NZ = 4, 4, 8
NROW = NX * NY
NCOL = NZ * 2
CELLS = 2 * NCOL * NROW
ENTITIES = NROW * NCOL * BLOCK
MESH = pl.DeviceIdType.MESH
F32 = jnp.float32
BF16 = jnp.bfloat16


def merge_kernel(
    chain, count, coords, seeds, tiles, cells, plan, product, slots, merged, rows, seed_rows, in_sem, out_sem, plan_sem
):
    order = (1, 2, 0)
    loads = {}
    for h in order:
        loads[h] = pltpu.make_async_copy(tiles.at[chain[h]], slots.at[h], in_sem.at[h])
        loads[h].start()
    lane = lax.broadcasted_iota(jnp.int32, (SLOTS, SLOTS), 1)
    line = lax.broadcasted_iota(jnp.int32, (SLOTS, SLOTS), 0)
    slot = lax.broadcasted_iota(jnp.int32, (1, SLOTS), 1)
    for h in range(HOPS):
        pair = coords[chain[h]]
        i, j = pair[0:1, :], pair[1:2, :]
        block = ((i >> 1) & 1) * 16 + (i >> 2) * 2 + (i & 1)
        if h == 0:
            word = block + (j << 8)
        else:
            key = jnp.where(slot < count[chain[h]], block * NROW + (j >> 1), CELLS + slot)
            keys = jnp.sum(jnp.where(lane == line, key, 0), axis=1, keepdims=True)
            first = jnp.min(jnp.where(keys == key, line, SLOTS), axis=0, keepdims=True)
            word = first + (jnp.where(first == slot, SLOTS, first) << 9) + ((j & 1) << 18)
            for n in range(CELLS // 128):
                cell = lane[:, :128] + n * 128
                found = jnp.where(keys == cell, line[:, :128], SLOTS)
                rows[h * 8 + n:h * 8 + n + 1, :] = jnp.min(found, axis=0, keepdims=True)
        for n in range(SLOTS // 128):
            rows[h * 8 + 4 + n:h * 8 + 5 + n, :] = word[:, n * 128:(n + 1) * 128]
    copy = pltpu.make_async_copy(rows, plan, plan_sem)
    copy.start()
    q = lax.axis_index("col")
    offsets = lax.broadcasted_iota(jnp.int32, (TILE, QUERIES), 0)
    for j in range(2 * NROW):
        ids = ((j // 2) * NCOL + q) * BLOCK + (j % 2) * TILE + offsets
        seed_rows[j] = jnp.where(ids == seeds[...], 1.0, 0.0).astype(BF16)
    product[...] = jnp.zeros_like(product)
    copy.wait()
    side_of = lax.broadcasted_iota(jnp.int32, (TILE, 2 * TILE), 1) >> 6
    stores = []
    for h in (1, 2):
        merged[h - 1, SLOTS] = jnp.zeros((TILE, 2 * TILE), F32)
        loads[h].wait()

        @pl.loop(0, count[chain[h]] // 32)
        def _(n):
            for u in range(16):
                value = slots[h, n * 16 + u]
                swapped = pltpu.roll(value, TILE, 1)
                for k in range(2):
                    t = n * 32 + u * 2 + k
                    word = plan[h * 8 + 4 + (t >> 7), t & 127]
                    side = word >> 18
                    base = merged[h - 1, (word >> 9) & 511]
                    moved = jnp.where(side == k, value, swapped)
                    merged[h - 1, word & 511] = base + jnp.where(side_of == side, moved, 0.0)

        copy = pltpu.make_async_copy(merged.at[h - 1], cells.at[h - 1], out_sem.at[h - 1])
        copy.start()
        stores.append(copy)
    loads[0].wait()
    none = jnp.zeros((TILE, QUERIES), BF16)

    @pl.loop(0, count[chain[0]] // 16)
    def _(n):
        for u in range(8):
            value = slots[0, n * 8 + u]
            top = value.astype(BF16)
            low = (value - top.astype(F32)).astype(BF16)
            t = n * 16 + u * 2
            words = [plan[4 + ((t + k) >> 7), (t + k) & 127] for k in range(2)]
            left = jnp.concatenate([seed_rows[words[0] >> 8], none], axis=0)
            right = jnp.concatenate([none, seed_rows[words[1] >> 8]], axis=0)
            both = jnp.dot(
                jnp.concatenate([top, low], axis=0), jnp.concatenate([left, right], axis=1), preferred_element_type=F32
            )
            both = both[:TILE] + both[TILE:]
            for k in range(2):
                at = words[k] & 255
                product[at] = product[at] + both[:, k * QUERIES:(k + 1) * QUERIES]

    for copy in stores:
        copy.wait()


def merge(chain, count, coords, seeds, tiles):
    smem = pl.BlockSpec(memory_space=pltpu.SMEM)
    vmem = pl.BlockSpec(memory_space=pltpu.VMEM)
    anywhere = pl.BlockSpec(memory_space=pl.ANY)
    return pl.pallas_call(
        merge_kernel,
        out_shape=(
            jax.ShapeDtypeStruct((HOPS - 1, SLOTS + 1, TILE, 2 * TILE), F32),
            jax.ShapeDtypeStruct((HOPS * 8, 128), jnp.int32),
            jax.ShapeDtypeStruct((2 * NCOL, TILE, QUERIES), F32),
        ),
        in_specs=[smem, smem, vmem, vmem, anywhere],
        out_specs=(anywhere, smem, vmem),
        scratch_shapes=[
            pltpu.VMEM((HOPS, SLOTS // 2, TILE, 2 * TILE), F32),
            pltpu.VMEM((HOPS - 1, SLOTS + 1, TILE, 2 * TILE), F32),
            pltpu.VMEM((HOPS * 8, 128), jnp.int32),
            pltpu.VMEM((2 * NROW, TILE, QUERIES), BF16),
            pltpu.SemaphoreType.DMA((HOPS,)),
            pltpu.SemaphoreType.DMA((HOPS - 1,)),
            pltpu.SemaphoreType.DMA,
        ],
        compiler_params=pltpu.CompilerParams(vmem_limit_bytes=48 * 2**20),
        name="first_hop_and_cells",
    )(chain, count, coords, seeds, tiles)


def chain_kernel(
    table, first, cells, out,
    held_a, held_b, dense_hi, dense_lo, right, part, cross, ring, state, col_tot, row_tot,
    load_sem, cross_sem, ring_sem, gather_sem, tot_sem,
):
    p = lax.axis_index("row")
    q = lax.axis_index("col")
    x, y = p // NY, p % NY
    z, core = q // 2, q % 2
    other = 1 - core
    held = (None, held_a, held_b)

    def remote(src, dst, send, recv, device):
        return pltpu.make_async_remote_copy(
            src_ref=src, dst_ref=dst, send_sem=send, recv_sem=recv, device_id=device, device_id_type=MESH
        )

    def load(h):
        return pltpu.make_async_copy(cells.at[h - 1], held[h], load_sem.at[h - 1])

    barrier = pltpu.get_barrier_semaphore()

    @pl.loop(1, 16)
    def _(d):
        pl.semaphore_signal(barrier, inc=1, device_id=(p, (q + d) % NCOL), device_id_type=MESH)
        pl.semaphore_signal(barrier, inc=1, device_id=((p + d) % NROW, q), device_id_type=MESH)

    load(1).start()
    load(2).start()

    def assemble(h, start, stop):
        @pl.loop(start, stop)
        def _(block):
            rows = pl.ds(pl.multiple_of(block * TILE, TILE), TILE)
            for s in range(NROW):
                value = held[h][table[h * 8 + (block >> 3), (block & 7) * NROW + s]]
                top = value.astype(BF16)
                dense_hi[s, rows, :] = top
                dense_lo[s, rows, :] = (value - top.astype(F32)).astype(BF16)

    def split(h, gx):
        for k in range(NY):
            value = state[h - 1, gx * NY + k]
            top = value.astype(BF16)
            right[k * BLOCK:(k + 1) * BLOCK, :QUERIES] = top
            right[k * BLOCK:(k + 1) * BLOCK, QUERIES:] = (value - top.astype(F32)).astype(BF16)

    def multiply(gx, half, fresh):
        @pl.loop(0, 2)
        def _(m):
            at = half * 8 + m * 4
            rows = pl.ds(pl.multiple_of(at * BLOCK, 4 * BLOCK), 4 * BLOCK)
            left = jnp.concatenate([dense_hi[gx * NY + k, rows, :] for k in range(NY)], axis=1)
            both = jnp.dot(left, right[...], preferred_element_type=F32)
            left = jnp.concatenate([dense_lo[gx * NY + k, rows, :] for k in range(NY)], axis=1)
            low = jnp.dot(left, right[:, :QUERIES], preferred_element_type=F32)
            total = (both[:, :QUERIES] + both[:, QUERIES:] + low).reshape(4, BLOCK, QUERIES)
            part[pl.ds(at, 4)] = total if fresh else part[pl.ds(at, 4)] + total

    def half_rows(u):
        return pl.ds(u * TILE, TILE)

    def away(way, k):
        return (z + (k if way == 0 else NZ - k)) % NZ

    pl.semaphore_wait(barrier, 30)
    sends = []

    def go(copy):
        copy.start()
        sends.append(copy)

    def block_at(h, u, source):
        return state.at[h, source, half_rows(u)]

    def across(u, d):
        return ((x + d) % NX) * NY + y if u == 0 else x * NY + (y + d) % NY

    def arrived(h, u, source):
        remote(
            block_at(h, u, source), block_at(h, u, source),
            gather_sem.at[0, h, u, 0], gather_sem.at[1, h, u, source], (p, z * 2 + other),
        ).wait_recv()

    for h in range(HOPS):
        whole = first if h == 0 else part

        def crossing(o):
            block = (z + o) % NZ
            return remote(
                whole.at[other * 8 + block], cross.at[h, block],
                cross_sem.at[0, h, o], cross_sem.at[1, h, o], (p, z * 2 + other),
            )

        order = (4, 3, 5, 1, 7, 2, 6, 0)
        if h > 0:
            groups = (0, 1, 3, 2)
            for n, d in enumerate(groups):
                gx = (x + d) % NX
                for u in range(2):
                    for e in range(NY):
                        if (e if u == 0 else d) != 0:
                            arrived(h - 1, u, gx * NY + (y + e) % NY)
                split(h, gx)
                multiply(gx, other, n == 0)
                if n == NX - 1:
                    for o in order:
                        copy = crossing(o)
                        copy.start()
                        crossed.append(copy)
                multiply(gx, core, n == 0)
        else:
            crossed = []
            for o in order:
                copy = crossing(o)
                copy.start()
                crossed.append(copy)

        def sum_of(o):
            return cross.at[h, (z + o) % NZ]

        def along(way, n, u, src, k):
            return remote(
                src, ring.at[h, way, n, half_rows(u)],
                ring_sem.at[0, h, way, n, u], ring_sem.at[1, h, way, n, u], (p, away(way, k) * 2 + core),
            )

        def got(way, n, u):
            along(way, n, u, ring.at[h, way, n, half_rows(u)], 1).wait_recv()

        for o in order:
            crossing(o).wait_recv()
            block = (z + o) % NZ
            cross[h, block] = cross[h, block] + whole[core * 8 + block]
            if o == 4:
                go(along(0, 3, 0, sum_of(4).at[half_rows(0)], 2))
                go(along(1, 3, 1, sum_of(4).at[half_rows(1)], 2))
            elif o in (3, 5):
                for u in range(2):
                    go(along(o // 4, 2, u, sum_of(o).at[half_rows(u)], 1))
            elif o in (1, 7):
                for u in range(2):
                    go(along(o // 4, 0, u, sum_of(o).at[half_rows(u)], 1))
        if h + 1 < HOPS:
            load(h + 1).wait()
            assemble(h + 1, 0, 16)
        for u in range(2):
            for way in range(2):
                got(way, 2, u)
                total = ring[h, way, 2, half_rows(u), :] + cross[h, away(way, 2), half_rows(u), :]
                if u == way:
                    got(way, 3, u)
                    total = total + ring[h, way, 3, half_rows(u), :]
                ring[h, way, 2, half_rows(u), :] = total
                go(along(way, 1, u, ring.at[h, way, 2, half_rows(u)], 2))
        if h + 1 < HOPS:
            assemble(h + 1, 16, 32)

        def finished(u):
            total = cross[h, z, half_rows(u), :]
            for n in (0, 1):
                for way in range(2):
                    got(way, n, u)
                    total = total + ring[h, way, n, half_rows(u), :]
            return total

        for copy in crossed:
            copy.wait_send()
        crossed = []
        if h + 1 < HOPS:
            used = [0, 0]

            def spread(u, source, device):
                go(remote(
                    block_at(h, u, source), block_at(h, u, source),
                    gather_sem.at[0, h, u, used[u]], gather_sem.at[1, h, u, source], device,
                ))
                used[u] += 1

            for u in range(2):
                state[h, p, half_rows(u), :] = finished(u)
                for d in (2, 1, 3):
                    spread(u, p, (across(u, d), q))
                for d in (2, 1, 3):
                    spread(u, p, (across(1 - u, d), q))
            for d in (1, 3, 2):
                for u in range(2):
                    arrived(h, u, across(u, d))
                    for e in (2, 1, 3):
                        spread(u, across(u, d), (x * NY + (y + e) % NY if u == 0 else ((x + e) % NX) * NY + y, q))
        else:
            for u in range(2):
                out[half_rows(u), :] = finished(u)

    owned = out[...]
    col_tot[q] = jnp.sum((owned * owned).reshape(16, 8, QUERIES), axis=0)

    def total(d, stage):
        if stage == 0:
            return remote(col_tot.at[q], col_tot.at[q], tot_sem.at[0, 0, d], tot_sem.at[1, 0, d], (p, (q + d) % NCOL))
        return remote(row_tot.at[p], row_tot.at[p], tot_sem.at[0, 1, d], tot_sem.at[1, 1, d], ((p + d) % NROW, q))

    for stage in range(2):
        @pl.loop(1, 16)
        def _(d):
            total(d, stage).start()

        @pl.loop(1, 16)
        def _(d):
            total(d, stage).wait()

        if stage == 0:
            row_tot[p] = jnp.sum(col_tot[...], axis=0)
    totals = jnp.sum(jnp.sum(row_tot[...], axis=0), axis=0, keepdims=True)
    out[...] = owned * lax.rsqrt(totals / ENTITIES + 1e-06)
    for copy in sends:
        copy.wait_send()


def run_chain(table, first, cells):
    smem = pl.BlockSpec(memory_space=pltpu.SMEM)
    vmem = pl.BlockSpec(memory_space=pltpu.VMEM)
    anywhere = pl.BlockSpec(memory_space=pl.ANY)
    return pl.pallas_call(
        chain_kernel,
        out_shape=jax.ShapeDtypeStruct((BLOCK, QUERIES), F32),
        in_specs=[smem, vmem, anywhere],
        out_specs=vmem,
        scratch_shapes=[
            pltpu.VMEM((SLOTS + 1, TILE, 2 * TILE), F32),
            pltpu.VMEM((SLOTS + 1, TILE, 2 * TILE), F32),
            pltpu.VMEM((NROW, NCOL * BLOCK, BLOCK), BF16),
            pltpu.VMEM((NROW, NCOL * BLOCK, BLOCK), BF16),
            pltpu.VMEM((NY * BLOCK, 2 * QUERIES), BF16),
            pltpu.VMEM((NCOL, BLOCK, QUERIES), F32),
            pltpu.VMEM((HOPS, NZ, BLOCK, QUERIES), F32),
            pltpu.VMEM((HOPS, 2, 4, BLOCK, QUERIES), F32),
            pltpu.VMEM((HOPS - 1, NROW, BLOCK, QUERIES), F32),
            pltpu.VMEM((NCOL, 8, QUERIES), F32),
            pltpu.VMEM((NROW, 8, QUERIES), F32),
            pltpu.SemaphoreType.DMA((HOPS - 1,)),
            pltpu.SemaphoreType.DMA((2, HOPS, NZ)),
            pltpu.SemaphoreType.DMA((2, HOPS, 2, 4, 2)),
            pltpu.SemaphoreType.DMA((2, HOPS - 1, 2, 16)),
            pltpu.SemaphoreType.DMA((2, 2, 16)),
        ],
        compiler_params=pltpu.CompilerParams(
            collective_id=0, has_side_effects=True, vmem_limit_bytes=54 * 2**20
        ),
        name="relation_chain",
    )(table, first, cells)


def shards(tiles, tile_coords, tile_count, seeds, chain):
    cells, table, product = merge(
        chain, tile_count[0, 0], tile_coords[0, 0], seeds.reshape(1, QUERIES), tiles[0, 0]
    )
    return run_chain(table, product.reshape(NCOL, BLOCK, QUERIES), cells)


def solution(mesh):
    in_specs = (
        P("row", "col", None, None, None, None),
        P("row", "col", None, None, None),
        P("row", "col", None),
        P(),
        P(),
    )
    out_specs = P(("row", "col"), None)
    return jax.shard_map(shards, mesh=mesh, in_specs=in_specs, out_specs=out_specs, check_vma=False)
```

time: 135 us -> 107 us (0.79)
  Pallas kernels: 134 us -> 101 us
  local copies, waits for them, and re-layouts: 1.47 us -> 5.71 us
    pallas_call x1, Pallas kernels: 114 us -> 90.3 us  [run_chain(): pl.pallas_call(chain_kernel, out_shape=jax.ShapeDtypeStruct((BLOCK, QUERI...]
    pallas_call x1, Pallas kernels: 19.4 us -> 10.4 us  [merge(): pl.pallas_call(merge_kernel, out_shape=(jax.ShapeDtypeStruct((HOPS - 1, S...]
    unnamed x1 -> x13, local copies, waits for them, and re-layouts: 1.47 us -> 5.71 us
where the time goes in v2:
time: 107 us; the launch traced here: 106 us
  Pallas kernels  101 us (94%)
  local copies, waits for them, and re-layouts  5.71 us (5%)
    pallas_call x1, Pallas kernels, run_chain(): pl.pallas_call(chain_kernel, out_shape=jax.ShapeDtypeStruct((BLOCK, QUERI...  90.3 us
    pallas_call x1, Pallas kernels, merge(): pl.pallas_call(merge_kernel, out_shape=(jax.ShapeDtypeStruct((HOPS - 1, S...  10.4 us
    unnamed x13, local copies, waits for them, and re-layouts  5.71 us

profile of v2, /device:TPU:1, one launch (start us, length us, event | category | flops | bytes accessed | tf_op | source)
XLA Modules:
  0.0 106.4 jit_solution(10235490169952036764)
XLA Ops:
  0.0 0.0 copy-start.2
  0.0 0.7 copy-done.2
  0.7 0.0 copy-start.3
  0.7 0.7 copy-done.3
  1.3 0.0 copy-start.4
  1.4 0.7 copy-done.4
  2.0 0.0 copy-start.5
  2.0 0.7 copy-done.5
  2.7 10.4 %first_hop_and_cells.1 = (f32[2,257,64,128]{3,2,1,0:T(8,128)}, s32[24,128]{1,0:T(8,128)S(1)}, f32[32,64,128]{2,1,0:T(8,128)S(1)}) custom-call(s32[3]{0:T(128)S(1)} %copy-done.3, s32[3]{0:T(128)S(1)} %bitcast.7, s32[3,2,256]{2,1,0:T(2,128)S(1)} %bitcast.6, s32[1,128]{1,0:T(1,128)S(1)} %bitcast.8, f32[3,128,64,128]{3,2,1,0:T(8,128)} %bitcast.9), custom_call_target="tpu_custom_call" | custom-call | tf_op jit(solution)/shard_map/first_hop_and_cells/pallas_call | solution.py:111
  13.1 0.0 copy-start
  13.1 1.0 copy-done
  14.1 0.0 copy-start.1
  14.1 0.6 copy-done.1
  14.7 90.3 %relation_chain.1 = f32[128,128]{1,0:T(8,128)} custom-call(s32[24,128]{1,0:T(8,128)} %copy-done.1, f32[16,128,128]{2,1,0:T(8,128)} %bitcast.5, f32[2,257,64,128]{3,2,1,0:T(8,128)} %get-tuple-element.10.cells), custom_call_target="tpu_custom_call" | custom-call | tf_op jit(solution)/shard_map/relation_chain/pallas_call | solution.py:357
  105.0 1.5 %copy.7 = f32[128,128]{1,0:T(8,128)} copy(f32[128,128]{1,0:T(8,128)} %relation_chain.1) | data formatting | bytes 131072
Async XLA Ops:
  0.0 0.7 copy-start.2
  0.7 0.7 copy-start.3
  1.3 0.7 copy-start.4
  2.0 0.7 copy-start.5
  13.1 1.0 copy-start
  14.1 0.6 copy-start.1

commit v3 on v2

--- a/solution.py
+++ b/solution.py
@@ -21,13 +21,22 @@
 
 
 def merge_kernel(
-    chain, count, coords, seeds, tiles, cells, plan, product, slots, merged, rows, seed_rows, in_sem, out_sem, plan_sem
+    chain_hbm, count_hbm, coords_hbm, seeds_hbm, tiles, cells, plan_hbm, product_hbm,
+    chain, count, coords, seeds, plan, product, slots, merged, rows, seed_rows, small_sem, in_sem, out_sem, plan_sem,
 ):
+    pairs = ((chain_hbm, chain), (count_hbm, count), (coords_hbm, coords), (seeds_hbm, seeds))
+    small = [pltpu.make_async_copy(src, dst, small_sem.at[n]) for n, (src, dst) in enumerate(pairs)]
+    for copy in small:
+        copy.start()
+    product[...] = jnp.zeros_like(product)
+    small[0].wait()
     order = (1, 2, 0)
     loads = {}
     for h in order:
         loads[h] = pltpu.make_async_copy(tiles.at[chain[h]], slots.at[h], in_sem.at[h])
         loads[h].start()
+    for copy in small[1:]:
+        copy.wait()
     lane = lax.broadcasted_iota(jnp.int32, (SLOTS, SLOTS), 1)
     line = lax.broadcasted_iota(jnp.int32, (SLOTS, SLOTS), 0)
     slot = lax.broadcasted_iota(jnp.int32, (1, SLOTS), 1)
@@ -48,17 +57,17 @@
                 rows[h * 8 + n:h * 8 + n + 1, :] = jnp.min(found, axis=0, keepdims=True)
         for n in range(SLOTS // 128):
             rows[h * 8 + 4 + n:h * 8 + 5 + n, :] = word[:, n * 128:(n + 1) * 128]
-    copy = pltpu.make_async_copy(rows, plan, plan_sem)
+    copy = pltpu.make_async_copy(rows, plan, plan_sem.at[0])
     copy.start()
+    stores = [pltpu.make_async_copy(rows, plan_hbm, plan_sem.at[1])]
+    stores[0].start()
     q = lax.axis_index("col")
     offsets = lax.broadcasted_iota(jnp.int32, (TILE, QUERIES), 0)
     for j in range(2 * NROW):
         ids = ((j // 2) * NCOL + q) * BLOCK + (j % 2) * TILE + offsets
         seed_rows[j] = jnp.where(ids == seeds[...], 1.0, 0.0).astype(BF16)
-    product[...] = jnp.zeros_like(product)
     copy.wait()
     side_of = lax.broadcasted_iota(jnp.int32, (TILE, 2 * TILE), 1) >> 6
-    stores = []
     for h in (1, 2):
         merged[h - 1, SLOTS] = jnp.zeros((TILE, 2 * TILE), F32)
         loads[h].wait()
@@ -100,14 +109,15 @@
                 at = words[k] & 255
                 product[at] = product[at] + both[:, k * QUERIES:(k + 1) * QUERIES]
 
+    copy = pltpu.make_async_copy(product, product_hbm, plan_sem.at[2])
+    copy.start()
+    stores.append(copy)
     for copy in stores:
         copy.wait()
 
 
 def merge(chain, count, coords, seeds, tiles):
-    smem = pl.BlockSpec(memory_space=pltpu.SMEM)
-    vmem = pl.BlockSpec(memory_space=pltpu.VMEM)
-    anywhere = pl.BlockSpec(memory_space=pl.ANY)
+    hbm = pl.BlockSpec(memory_space=pltpu.HBM)
     return pl.pallas_call(
         merge_kernel,
         out_shape=(
@@ -115,26 +125,33 @@
             jax.ShapeDtypeStruct((HOPS * 8, 128), jnp.int32),
             jax.ShapeDtypeStruct((2 * NCOL, TILE, QUERIES), F32),
         ),
-        in_specs=[smem, smem, vmem, vmem, anywhere],
-        out_specs=(anywhere, smem, vmem),
+        in_specs=[hbm] * 5,
+        out_specs=(hbm, hbm, hbm),
         scratch_shapes=[
+            pltpu.SMEM((HOPS,), jnp.int32),
+            pltpu.SMEM((HOPS,), jnp.int32),
+            pltpu.VMEM((HOPS, 2, SLOTS), jnp.int32),
+            pltpu.VMEM((1, QUERIES), jnp.int32),
+            pltpu.SMEM((HOPS * 8, 128), jnp.int32),
+            pltpu.VMEM((2 * NCOL, TILE, QUERIES), F32),
             pltpu.VMEM((HOPS, SLOTS // 2, TILE, 2 * TILE), F32),
             pltpu.VMEM((HOPS - 1, SLOTS + 1, TILE, 2 * TILE), F32),
             pltpu.VMEM((HOPS * 8, 128), jnp.int32),
             pltpu.VMEM((2 * NROW, TILE, QUERIES), BF16),
+            pltpu.SemaphoreType.DMA((4,)),
             pltpu.SemaphoreType.DMA((HOPS,)),
             pltpu.SemaphoreType.DMA((HOPS - 1,)),
-            pltpu.SemaphoreType.DMA,
+            pltpu.SemaphoreType.DMA((3,)),
         ],
-        compiler_params=pltpu.CompilerParams(vmem_limit_bytes=48 * 2**20),
+        compiler_params=pltpu.CompilerParams(vmem_limit_bytes=60 * 2**20),
         name="first_hop_and_cells",
     )(chain, count, coords, seeds, tiles)
 
 
 def chain_kernel(
-    table, first, cells, out,
-    held_a, held_b, dense_hi, dense_lo, right, part, cross, ring, state, col_tot, row_tot,
-    load_sem, cross_sem, ring_sem, gather_sem, tot_sem,
+    table_hbm, first, cells, out,
+    table, held_a, held_b, dense_hi, dense_lo, right, part, cross, ring, state, col_tot, row_tot,
+    load_sem, sent_sem, cross_sem, ring_sem, gather_sem, tot_sem,
 ):
     p = lax.axis_index("row")
     q = lax.axis_index("col")
@@ -158,6 +175,11 @@
         pl.semaphore_signal(barrier, inc=1, device_id=(p, (q + d) % NCOL), device_id_type=MESH)
         pl.semaphore_signal(barrier, inc=1, device_id=((p + d) % NROW, q), device_id_type=MESH)
 
+    fetches = [
+        pltpu.make_async_copy(first, part, load_sem.at[2]), pltpu.make_async_copy(table_hbm, table, load_sem.at[3]),
+    ]
+    for copy in fetches:
+        copy.start()
     load(1).start()
     load(2).start()
 
@@ -196,12 +218,12 @@
     def away(way, k):
         return (z + (k if way == 0 else NZ - k)) % NZ
 
+    for copy in fetches:
+        copy.wait()
     pl.semaphore_wait(barrier, 30)
-    sends = []
-
-    def go(copy):
-        copy.start()
-        sends.append(copy)
+
+    def sent(kind, h, ref):
+        remote(ref, ref, sent_sem.at[kind, h], sent_sem.at[kind, h], (p, z * 2 + other)).wait_send()
 
     def block_at(h, u, source):
         return state.at[h, source, half_rows(u)]
@@ -212,17 +234,16 @@
     def arrived(h, u, source):
         remote(
             block_at(h, u, source), block_at(h, u, source),
-            gather_sem.at[0, h, u, 0], gather_sem.at[1, h, u, source], (p, z * 2 + other),
+            sent_sem.at[1, h], gather_sem.at[h, u, source], (p, z * 2 + other),
         ).wait_recv()
 
     for h in range(HOPS):
-        whole = first if h == 0 else part
 
         def crossing(o):
             block = (z + o) % NZ
             return remote(
-                whole.at[other * 8 + block], cross.at[h, block],
-                cross_sem.at[0, h, o], cross_sem.at[1, h, o], (p, z * 2 + other),
+                part.at[other * 8 + block], cross.at[h, block],
+                sent_sem.at[0, h], cross_sem.at[h, o], (p, z * 2 + other),
             )
 
         order = (4, 3, 5, 1, 7, 2, 6, 0)
@@ -238,16 +259,11 @@
                 multiply(gx, other, n == 0)
                 if n == NX - 1:
                     for o in order:
-                        copy = crossing(o)
-                        copy.start()
-                        crossed.append(copy)
+                        crossing(o).start()
                 multiply(gx, core, n == 0)
         else:
-            crossed = []
             for o in order:
-                copy = crossing(o)
-                copy.start()
-                crossed.append(copy)
+                crossing(o).start()
 
         def sum_of(o):
             return cross.at[h, (z + o) % NZ]
@@ -255,7 +271,7 @@
         def along(way, n, u, src, k):
             return remote(
                 src, ring.at[h, way, n, half_rows(u)],
-                ring_sem.at[0, h, way, n, u], ring_sem.at[1, h, way, n, u], (p, away(way, k) * 2 + core),
+                sent_sem.at[2, h], ring_sem.at[h, way, n, u], (p, away(way, k) * 2 + core),
             )
 
         def got(way, n, u):
@@ -264,16 +280,16 @@
         for o in order:
             crossing(o).wait_recv()
             block = (z + o) % NZ
-            cross[h, block] = cross[h, block] + whole[core * 8 + block]
+            cross[h, block] = cross[h, block] + part[core * 8 + block]
             if o == 4:
-                go(along(0, 3, 0, sum_of(4).at[half_rows(0)], 2))
-                go(along(1, 3, 1, sum_of(4).at[half_rows(1)], 2))
+                along(0, 3, 0, sum_of(4).at[half_rows(0)], 2).start()
+                along(1, 3, 1, sum_of(4).at[half_rows(1)], 2).start()
             elif o in (3, 5):
                 for u in range(2):
-                    go(along(o // 4, 2, u, sum_of(o).at[half_rows(u)], 1))
+                    along(o // 4, 2, u, sum_of(o).at[half_rows(u)], 1).start()
             elif o in (1, 7):
                 for u in range(2):
-                    go(along(o // 4, 0, u, sum_of(o).at[half_rows(u)], 1))
+                    along(o // 4, 0, u, sum_of(o).at[half_rows(u)], 1).start()
         if h + 1 < HOPS:
             load(h + 1).wait()
             assemble(h + 1, 0, 16)
@@ -285,7 +301,7 @@
                     got(way, 3, u)
                     total = total + ring[h, way, 3, half_rows(u), :]
                 ring[h, way, 2, half_rows(u), :] = total
-                go(along(way, 1, u, ring.at[h, way, 2, half_rows(u)], 2))
+                along(way, 1, u, ring.at[h, way, 2, half_rows(u)], 2).start()
         if h + 1 < HOPS:
             assemble(h + 1, 16, 32)
 
@@ -297,18 +313,13 @@
                     total = total + ring[h, way, n, half_rows(u), :]
             return total
 
-        for copy in crossed:
-            copy.wait_send()
-        crossed = []
+        sent(0, h, part.at[pl.ds(0, NZ)])
         if h + 1 < HOPS:
-            used = [0, 0]
-
             def spread(u, source, device):
-                go(remote(
+                remote(
                     block_at(h, u, source), block_at(h, u, source),
-                    gather_sem.at[0, h, u, used[u]], gather_sem.at[1, h, u, source], device,
-                ))
-                used[u] += 1
+                    sent_sem.at[1, h], gather_sem.at[h, u, source], device,
+                ).start()
 
             for u in range(2):
                 state[h, p, half_rows(u), :] = finished(u)
@@ -328,38 +339,33 @@
     owned = out[...]
     col_tot[q] = jnp.sum((owned * owned).reshape(16, 8, QUERIES), axis=0)
 
-    def total(d, stage):
-        if stage == 0:
-            return remote(col_tot.at[q], col_tot.at[q], tot_sem.at[0, 0, d], tot_sem.at[1, 0, d], (p, (q + d) % NCOL))
-        return remote(row_tot.at[p], row_tot.at[p], tot_sem.at[0, 1, d], tot_sem.at[1, 1, d], ((p + d) % NROW, q))
-
-    for stage in range(2):
-        @pl.loop(1, 16)
-        def _(d):
-            total(d, stage).start()
-
-        @pl.loop(1, 16)
-        def _(d):
-            total(d, stage).wait()
-
+    far_first = (8, 7, 9, 6, 10, 5, 11, 4, 12, 3, 13, 2, 14, 1, 15)
+    for stage, (tot, me) in enumerate(((col_tot, q), (row_tot, p))):
+        for d in far_first:
+            device = (p, (q + d) % NCOL) if stage == 0 else ((p + d) % NROW, q)
+            remote(tot.at[me], tot.at[me], tot_sem.at[0, stage], tot_sem.at[1, stage], device).start()
+        every = tot.at[pl.ds(0, 15)]
+        remote(every, every, tot_sem.at[0, stage], tot_sem.at[1, stage], (p, z * 2 + other)).wait()
         if stage == 0:
             row_tot[p] = jnp.sum(col_tot[...], axis=0)
     totals = jnp.sum(jnp.sum(row_tot[...], axis=0), axis=0, keepdims=True)
     out[...] = owned * lax.rsqrt(totals / ENTITIES + 1e-06)
-    for copy in sends:
-        copy.wait_send()
+    for h in range(HOPS):
+        sent(2, h, cross.at[0, pl.ds(0, 7)])
+    for h in range(HOPS - 1):
+        sent(1, h, state.at[0, pl.ds(0, NROW - 1)])
 
 
 def run_chain(table, first, cells):
-    smem = pl.BlockSpec(memory_space=pltpu.SMEM)
     vmem = pl.BlockSpec(memory_space=pltpu.VMEM)
-    anywhere = pl.BlockSpec(memory_space=pl.ANY)
+    hbm = pl.BlockSpec(memory_space=pltpu.HBM)
     return pl.pallas_call(
         chain_kernel,
         out_shape=jax.ShapeDtypeStruct((BLOCK, QUERIES), F32),
-        in_specs=[smem, vmem, anywhere],
+        in_specs=[hbm] * 3,
         out_specs=vmem,
         scratch_shapes=[
+            pltpu.SMEM((HOPS * 8, 128), jnp.int32),
             pltpu.VMEM((SLOTS + 1, TILE, 2 * TILE), F32),
             pltpu.VMEM((SLOTS + 1, TILE, 2 * TILE), F32),
             pltpu.VMEM((NROW, NCOL * BLOCK, BLOCK), BF16),
@@ -371,14 +377,15 @@
             pltpu.VMEM((HOPS - 1, NROW, BLOCK, QUERIES), F32),
             pltpu.VMEM((NCOL, 8, QUERIES), F32),
             pltpu.VMEM((NROW, 8, QUERIES), F32),
-            pltpu.SemaphoreType.DMA((HOPS - 1,)),
-            pltpu.SemaphoreType.DMA((2, HOPS, NZ)),
-            pltpu.SemaphoreType.DMA((2, HOPS, 2, 4, 2)),
-            pltpu.SemaphoreType.DMA((2, HOPS - 1, 2, 16)),
-            pltpu.SemaphoreType.DMA((2, 2, 16)),
+            pltpu.SemaphoreType.DMA((4,)),
+            pltpu.SemaphoreType.DMA((3, HOPS)),
+            pltpu.SemaphoreType.DMA((HOPS, NZ)),
+            pltpu.SemaphoreType.DMA((HOPS, 2, 4, 2)),
+            pltpu.SemaphoreType.DMA((HOPS - 1, 2, 16)),
+            pltpu.SemaphoreType.DMA((2, 2)),
         ],
         compiler_params=pltpu.CompilerParams(
-            collective_id=0, has_side_effects=True, vmem_limit_bytes=54 * 2**20
+            collective_id=0, has_side_effects=True, vmem_limit_bytes=60 * 2**20
         ),
         name="relation_chain",
     )(table, first, cells)

time: 107 us -> 98.6 us (0.921)
  local copies, waits for them, and re-layouts: 5.71 us -> 1.47 us
  Pallas kernels: 101 us -> 97 us
    pallas_call x1, Pallas kernels: 90.3 us -> 84.8 us  [run_chain(): pl.pallas_call(chain_kernel, out_shape=jax.ShapeDtypeStruct((BLOCK, QUERI...]
    unnamed x13 -> x1, local copies, waits for them, and re-layouts: 5.71 us -> 1.47 us
    pallas_call x1, Pallas kernels: 10.4 us -> 12.2 us  [merge(): pl.pallas_call(merge_kernel, out_shape=(jax.ShapeDtypeStruct((HOPS - 1, S...]
where the time goes in v3:
time: 98.6 us; the launch traced here: 98.4 us
  Pallas kernels  97 us (98%)
  local copies, waits for them, and re-layouts  1.47 us (1%)
    pallas_call x1, Pallas kernels, run_chain(): pl.pallas_call(chain_kernel, out_shape=jax.ShapeDtypeStruct((BLOCK, QUERI...  84.8 us
    pallas_call x1, Pallas kernels, merge(): pl.pallas_call(merge_kernel, out_shape=(jax.ShapeDtypeStruct((HOPS - 1, S...  12.2 us

profile of v3, /device:TPU:1, one launch (start us, length us, event | category | flops | bytes accessed | tf_op | source)
XLA Modules:
  0.0 98.4 jit_solution(8024364968131126030)
XLA Ops:
  0.0 12.2 %first_hop_and_cells.1 = (f32[2,257,64,128]{3,2,1,0:T(8,128)}, s32[24,128]{1,0:T(8,128)}, f32[32,64,128]{2,1,0:T(8,128)}) custom-call(s32[3]{0:T(128)} %chain_hbm.1, s32[3]{0:T(128)} %bitcast.8, s32[3,2,256]{2,1,0:T(2,128)} %bitcast.7, s32[1,128]{1,0:T(1,128)} %bitcast.9, f32[3,128,64,128]{3,2,1,0:T(8,128)} %bitcast.5), custom_call_target="tpu_custom_call" | custom-call | tf_op jit(solution)/shard_map/first_hop_and_cells/pallas_call | solution.py:121
  12.2 84.8 %relation_chain.1 = f32[128,128]{1,0:T(8,128)} custom-call(s32[24,128]{1,0:T(8,128)} %get-tuple-element.8.table_hbm, f32[16,128,128]{2,1,0:T(8,128)} %bitcast.6, f32[2,257,64,128]{3,2,1,0:T(8,128)} %get-tuple-element.10.cells), custom_call_target="tpu_custom_call" | custom-call | tf_op jit(solution)/shard_map/relation_chain/pallas_call | solution.py:362
  97.0 1.5 %copy.7 = f32[128,128]{1,0:T(8,128)} copy(f32[128,128]{1,0:T(8,128)} %relation_chain.1) | data formatting | bytes 131072

commit v4 on v3

--- a/solution.py
+++ b/solution.py
@@ -47,10 +47,14 @@
         if h == 0:
             word = block + (j << 8)
         else:
-            key = jnp.where(slot < count[chain[h]], block * NROW + (j >> 1), CELLS + slot)
+            along_x, along_y = j >> 3, (j >> 1) & 3
+            second = (j & 1) == 1
+            couple = jnp.where(second, 8 + along_y * 2 + (along_x >> 1), along_x * 2 + (along_y >> 1))
+            side = jnp.where(second, along_x & 1, along_y & 1)
+            key = jnp.where(slot < count[chain[h]], block * NROW + couple, CELLS + slot)
             keys = jnp.sum(jnp.where(lane == line, key, 0), axis=1, keepdims=True)
             first = jnp.min(jnp.where(keys == key, line, SLOTS), axis=0, keepdims=True)
-            word = first + (jnp.where(first == slot, SLOTS, first) << 9) + ((j & 1) << 18)
+            word = first + (jnp.where(first == slot, SLOTS, first) << 9) + (side << 18)
             for n in range(CELLS // 128):
                 cell = lane[:, :128] + n * 128
                 found = jnp.where(keys == cell, line[:, :128], SLOTS)
@@ -193,24 +197,30 @@
                 dense_hi[s, rows, :] = top
                 dense_lo[s, rows, :] = (value - top.astype(F32)).astype(BF16)
 
-    def split(h, gx):
-        for k in range(NY):
-            value = state[h - 1, gx * NY + k]
-            top = value.astype(BF16)
-            right[k * BLOCK:(k + 1) * BLOCK, :QUERIES] = top
-            right[k * BLOCK:(k + 1) * BLOCK, QUERIES:] = (value - top.astype(F32)).astype(BF16)
-
-    def multiply(gx, half, fresh):
-        @pl.loop(0, 2)
+    def split(h, d):
+        gx, gy = (x + d) % NX, (y + d) % NY
+        for u in range(2):
+            for k in range(NX):
+                value = state[h - 1, gx * NY + k if u == 0 else k * NY + gy, u * TILE:(u + 1) * TILE, :]
+                top = value.astype(BF16)
+                at = (u * NX + k) * TILE
+                right[at:at + TILE, :QUERIES] = top
+                right[at:at + TILE, QUERIES:] = (value - top.astype(F32)).astype(BF16)
+
+    def multiply(d, start, steps):
+        gx, gy = (x + d) % NX, (y + d) % NY
+        couples = (gx * 2, gx * 2 + 1, 8 + gy * 2, 9 + gy * 2)
+
+        @pl.loop(0, steps)
         def _(m):
-            at = half * 8 + m * 4
-            rows = pl.ds(pl.multiple_of(at * BLOCK, 4 * BLOCK), 4 * BLOCK)
-            left = jnp.concatenate([dense_hi[gx * NY + k, rows, :] for k in range(NY)], axis=1)
+            at = start + m * 8
+            rows = pl.ds(pl.multiple_of(at * BLOCK, 8 * BLOCK), 8 * BLOCK)
+            left = jnp.concatenate([dense_hi[c, rows, :] for c in couples], axis=1)
             both = jnp.dot(left, right[...], preferred_element_type=F32)
-            left = jnp.concatenate([dense_lo[gx * NY + k, rows, :] for k in range(NY)], axis=1)
+            left = jnp.concatenate([dense_lo[c, rows, :] for c in couples], axis=1)
             low = jnp.dot(left, right[:, :QUERIES], preferred_element_type=F32)
-            total = (both[:, :QUERIES] + both[:, QUERIES:] + low).reshape(4, BLOCK, QUERIES)
-            part[pl.ds(at, 4)] = total if fresh else part[pl.ds(at, 4)] + total
+            total = both[:, :QUERIES] + both[:, QUERIES:] + low
+            part[pl.ds(at, 8)] = part[pl.ds(at, 8)] + total.reshape(8, BLOCK, QUERIES)
 
     def half_rows(u):
         return pl.ds(u * TILE, TILE)
@@ -248,19 +258,24 @@
 
         order = (4, 3, 5, 1, 7, 2, 6, 0)
         if h > 0:
-            groups = (0, 1, 3, 2)
-            for n, d in enumerate(groups):
-                gx = (x + d) % NX
-                for u in range(2):
-                    for e in range(NY):
-                        if (e if u == 0 else d) != 0:
-                            arrived(h - 1, u, gx * NY + (y + e) % NY)
-                split(h, gx)
-                multiply(gx, other, n == 0)
-                if n == NX - 1:
-                    for o in order:
-                        crossing(o).start()
-                multiply(gx, core, n == 0)
+            def columns(d):
+                for e in (1, 2, 3):
+                    arrived(h - 1, 0, ((x + d) % NX) * NY + (y + e) % NY)
+                    arrived(h - 1, 1, ((x + e) % NX) * NY + (y + d) % NY)
+                split(h, d)
+
+            part[...] = jnp.zeros_like(part)
+
+            @pl.loop(0, NX - 1)
+            def _(n):
+                columns(n + n // 2)
+                multiply(n + n // 2, 0, 2)
+
+            columns(2)
+            multiply(2, other * 8, 1)
+            for o in order:
+                crossing(o).start()
+            multiply(2, core * 8, 1)
         else:
             for o in order:
                 crossing(o).start()
@@ -323,14 +338,14 @@
 
             for u in range(2):
                 state[h, p, half_rows(u), :] = finished(u)
-                for d in (2, 1, 3):
+                for d in (1, 3, 2):
                     spread(u, p, (across(u, d), q))
-                for d in (2, 1, 3):
+                for d in (1, 3, 2):
                     spread(u, p, (across(1 - u, d), q))
             for d in (1, 3, 2):
                 for u in range(2):
                     arrived(h, u, across(u, d))
-                    for e in (2, 1, 3):
+                    for e in (1, 3, 2):
                         spread(u, across(u, d), (x * NY + (y + e) % NY if u == 0 else ((x + e) % NX) * NY + y, q))
         else:
             for u in range(2):

time: 98.6 us -> 95.3 us (0.967)
  Pallas kernels: 97 us -> 93.6 us
    pallas_call x1, Pallas kernels: 84.8 us -> 81.2 us  [run_chain(): pl.pallas_call(chain_kernel, out_shape=jax.ShapeDtypeStruct((BLOCK, QUERI...]
where the time goes in v4:
time: 95.3 us; the launch traced here: 95.1 us
  Pallas kernels  93.6 us (98%)
  local copies, waits for them, and re-layouts  1.47 us (2%)
    pallas_call x1, Pallas kernels, run_chain(): pl.pallas_call(chain_kernel, out_shape=jax.ShapeDtypeStruct((BLOCK, QUERI...  81.2 us
    pallas_call x1, Pallas kernels, merge(): pl.pallas_call(merge_kernel, out_shape=(jax.ShapeDtypeStruct((HOPS - 1, S...  12.4 us

profile of v4, /device:TPU:1, one launch (start us, length us, event | category | flops | bytes accessed | tf_op | source)
XLA Modules:
  0.0 95.1 jit_solution(6274495105761866291)
XLA Ops:
  0.0 12.4 %first_hop_and_cells.1 = (f32[2,257,64,128]{3,2,1,0:T(8,128)}, s32[24,128]{1,0:T(8,128)}, f32[32,64,128]{2,1,0:T(8,128)}) custom-call(s32[3]{0:T(128)} %chain_hbm.1, s32[3]{0:T(128)} %bitcast.8, s32[3,2,256]{2,1,0:T(2,128)} %bitcast.7, s32[1,128]{1,0:T(1,128)} %bitcast.9, f32[3,128,64,128]{3,2,1,0:T(8,128)} %bitcast.5), custom_call_target="tpu_custom_call" | custom-call | tf_op jit(solution)/shard_map/first_hop_and_cells/pallas_call | solution.py:125
  12.4 81.2 %relation_chain.1 = f32[128,128]{1,0:T(8,128)} custom-call(s32[24,128]{1,0:T(8,128)} %get-tuple-element.8.table_hbm, f32[16,128,128]{2,1,0:T(8,128)} %bitcast.6, f32[2,257,64,128]{3,2,1,0:T(8,128)} %get-tuple-element.10.cells), custom_call_target="tpu_custom_call" | custom-call | tf_op jit(solution)/shard_map/relation_chain/pallas_call | solution.py:377
  93.6 1.5 %copy.7 = f32[128,128]{1,0:T(8,128)} copy(f32[128,128]{1,0:T(8,128)} %relation_chain.1) | data formatting | bytes 131072

commit v5 on v4

--- a/solution.py
+++ b/solution.py
@@ -95,13 +95,13 @@
     loads[0].wait()
     none = jnp.zeros((TILE, QUERIES), BF16)
 
-    @pl.loop(0, count[chain[0]] // 16)
+    @pl.loop(0, count[chain[0]] // 32)
     def _(n):
-        for u in range(8):
-            value = slots[0, n * 8 + u]
+        for u in range(16):
+            value = slots[0, n * 16 + u]
             top = value.astype(BF16)
             low = (value - top.astype(F32)).astype(BF16)
-            t = n * 16 + u * 2
+            t = n * 32 + u * 2
             words = [plan[4 + ((t + k) >> 7), (t + k) & 127] for k in range(2)]
             left = jnp.concatenate([seed_rows[words[0] >> 8], none], axis=0)
             right = jnp.concatenate([none, seed_rows[words[1] >> 8]], axis=0)
@@ -155,7 +155,7 @@
 def chain_kernel(
     table_hbm, first, cells, out,
     table, held_a, held_b, dense_hi, dense_lo, right, part, cross, ring, state, col_tot, row_tot,
-    load_sem, sent_sem, cross_sem, ring_sem, gather_sem, tot_sem,
+    load_sem, sent_sem, cross_sem, ring_sem, first_sem, group_sem, tot_sem,
 ):
     p = lax.axis_index("row")
     q = lax.axis_index("col")
@@ -241,11 +241,13 @@
     def across(u, d):
         return ((x + d) % NX) * NY + y if u == 0 else x * NY + (y + d) % NY
 
-    def arrived(h, u, source):
-        remote(
-            block_at(h, u, source), block_at(h, u, source),
-            sent_sem.at[1, h], gather_sem.at[h, u, source], (p, z * 2 + other),
-        ).wait_recv()
+    def arrived(h, u, d):
+        source = block_at(h, u, across(u, d))
+        remote(source, source, sent_sem.at[1, h], first_sem.at[h, u, d - 1], (p, z * 2 + other)).wait_recv()
+
+    def group_arrived(h, d):
+        six = state.at[h, pl.ds(0, 3)]
+        remote(six, six, sent_sem.at[1, h], group_sem.at[h, d], (p, z * 2 + other)).wait_recv()
 
     for h in range(HOPS):
 
@@ -259,9 +261,7 @@
         order = (4, 3, 5, 1, 7, 2, 6, 0)
         if h > 0:
             def columns(d):
-                for e in (1, 2, 3):
-                    arrived(h - 1, 0, ((x + d) % NX) * NY + (y + e) % NY)
-                    arrived(h - 1, 1, ((x + e) % NX) * NY + (y + d) % NY)
+                group_arrived(h - 1, d)
                 split(h, d)
 
             part[...] = jnp.zeros_like(part)
@@ -330,40 +330,39 @@
 
         sent(0, h, part.at[pl.ds(0, NZ)])
         if h + 1 < HOPS:
-            def spread(u, source, device):
-                remote(
-                    block_at(h, u, source), block_at(h, u, source),
-                    sent_sem.at[1, h], gather_sem.at[h, u, source], device,
-                ).start()
+            def spread(u, source, device, arrival):
+                block = block_at(h, u, source)
+                remote(block, block, sent_sem.at[1, h], arrival, (device, q)).start()
 
             for u in range(2):
                 state[h, p, half_rows(u), :] = finished(u)
                 for d in (1, 3, 2):
-                    spread(u, p, (across(u, d), q))
-                for d in (1, 3, 2):
-                    spread(u, p, (across(1 - u, d), q))
+                    spread(u, p, across(u, d), first_sem.at[h, u, NX - d - 1])
+                for e in (1, 3, 2):
+                    spread(u, p, across(1 - u, e), group_sem.at[h, 0])
             for d in (1, 3, 2):
                 for u in range(2):
-                    arrived(h, u, across(u, d))
+                    arrived(h, u, d)
                     for e in (1, 3, 2):
-                        spread(u, across(u, d), (x * NY + (y + e) % NY if u == 0 else ((x + e) % NX) * NY + y, q))
+                        spread(u, across(u, d), across(1 - u, e), group_sem.at[h, d])
         else:
             for u in range(2):
                 out[half_rows(u), :] = finished(u)
 
     owned = out[...]
-    col_tot[q] = jnp.sum((owned * owned).reshape(16, 8, QUERIES), axis=0)
+    top_row = pl.ds(0, 1)
+    col_tot[q, top_row, :] = jnp.sum(owned * owned, axis=0, keepdims=True)
 
     far_first = (8, 7, 9, 6, 10, 5, 11, 4, 12, 3, 13, 2, 14, 1, 15)
     for stage, (tot, me) in enumerate(((col_tot, q), (row_tot, p))):
         for d in far_first:
             device = (p, (q + d) % NCOL) if stage == 0 else ((p + d) % NROW, q)
-            remote(tot.at[me], tot.at[me], tot_sem.at[0, stage], tot_sem.at[1, stage], device).start()
-        every = tot.at[pl.ds(0, 15)]
+            remote(tot.at[me, top_row], tot.at[me, top_row], tot_sem.at[0, stage], tot_sem.at[1, stage], device).start()
+        every = tot.at[pl.ds(0, 15), top_row]
         remote(every, every, tot_sem.at[0, stage], tot_sem.at[1, stage], (p, z * 2 + other)).wait()
         if stage == 0:
-            row_tot[p] = jnp.sum(col_tot[...], axis=0)
-    totals = jnp.sum(jnp.sum(row_tot[...], axis=0), axis=0, keepdims=True)
+            row_tot[p, top_row, :] = jnp.sum(col_tot[:, top_row, :], axis=0)
+    totals = jnp.sum(row_tot[:, top_row, :], axis=0)
     out[...] = owned * lax.rsqrt(totals / ENTITIES + 1e-06)
     for h in range(HOPS):
         sent(2, h, cross.at[0, pl.ds(0, 7)])
@@ -396,7 +395,8 @@
             pltpu.SemaphoreType.DMA((3, HOPS)),
             pltpu.SemaphoreType.DMA((HOPS, NZ)),
             pltpu.SemaphoreType.DMA((HOPS, 2, 4, 2)),
-            pltpu.SemaphoreType.DMA((HOPS - 1, 2, 16)),
+            pltpu.SemaphoreType.DMA((HOPS - 1, 2, NX - 1)),
+            pltpu.SemaphoreType.DMA((HOPS - 1, NX)),
             pltpu.SemaphoreType.DMA((2, 2)),
         ],
         compiler_params=pltpu.CompilerParams(

time: 95.3 us -> 92 us (0.965)
  Pallas kernels: 93.6 us -> 90.3 us
    pallas_call x1, Pallas kernels: 12.4 us -> 10.2 us  [merge(): pl.pallas_call(merge_kernel, out_shape=(jax.ShapeDtypeStruct((HOPS - 1, S...]
    pallas_call x1, Pallas kernels: 81.2 us -> 80.1 us  [run_chain(): pl.pallas_call(chain_kernel, out_shape=jax.ShapeDtypeStruct((BLOCK, QUERI...]
where the time goes in v5:
time: 92 us; the launch traced here: 91.8 us
  Pallas kernels  90.3 us (98%)
  local copies, waits for them, and re-layouts  1.47 us (2%)
    pallas_call x1, Pallas kernels, run_chain(): pl.pallas_call(chain_kernel, out_shape=jax.ShapeDtypeStruct((BLOCK, QUERI...  80.1 us
    pallas_call x1, Pallas kernels, merge(): pl.pallas_call(merge_kernel, out_shape=(jax.ShapeDtypeStruct((HOPS - 1, S...  10.2 us

profile of v5, /device:TPU:1, one launch (start us, length us, event | category | flops | bytes accessed | tf_op | source)
XLA Modules:
  0.0 91.8 jit_solution(5936805189475273583)
XLA Ops:
  0.0 10.2 %first_hop_and_cells.1 = (f32[2,257,64,128]{3,2,1,0:T(8,128)}, s32[24,128]{1,0:T(8,128)}, f32[32,64,128]{2,1,0:T(8,128)}) custom-call(s32[3]{0:T(128)} %chain_hbm.1, s32[3]{0:T(128)} %bitcast.8, s32[3,2,256]{2,1,0:T(2,128)} %bitcast.7, s32[1,128]{1,0:T(1,128)} %bitcast.9, f32[3,128,64,128]{3,2,1,0:T(8,128)} %bitcast.5), custom_call_target="tpu_custom_call" | custom-call | tf_op jit(solution)/shard_map/first_hop_and_cells/pallas_call | solution.py:125
  10.3 80.1 %relation_chain.1 = f32[128,128]{1,0:T(8,128)} custom-call(s32[24,128]{1,0:T(8,128)} %get-tuple-element.8.table_hbm, f32[16,128,128]{2,1,0:T(8,128)} %bitcast.6, f32[2,257,64,128]{3,2,1,0:T(8,128)} %get-tuple-element.10.cells), custom_call_target="tpu_custom_call" | custom-call | tf_op jit(solution)/shard_map/relation_chain/pallas_call | solution.py:376
  90.4 1.5 %copy.7 = f32[128,128]{1,0:T(8,128)} copy(f32[128,128]{1,0:T(8,128)} %relation_chain.1) | data formatting | bytes 131072

commit v6 on v5

--- a/solution.py
+++ b/solution.py
@@ -207,20 +207,20 @@
                 right[at:at + TILE, :QUERIES] = top
                 right[at:at + TILE, QUERIES:] = (value - top.astype(F32)).astype(BF16)
 
-    def multiply(d, start, steps):
+    def multiply(d, start, steps, size=8):
         gx, gy = (x + d) % NX, (y + d) % NY
         couples = (gx * 2, gx * 2 + 1, 8 + gy * 2, 9 + gy * 2)
 
         @pl.loop(0, steps)
         def _(m):
-            at = start + m * 8
-            rows = pl.ds(pl.multiple_of(at * BLOCK, 8 * BLOCK), 8 * BLOCK)
+            at = start + m * size
+            rows = pl.ds(pl.multiple_of(at * BLOCK, size * BLOCK), size * BLOCK)
             left = jnp.concatenate([dense_hi[c, rows, :] for c in couples], axis=1)
             both = jnp.dot(left, right[...], preferred_element_type=F32)
             left = jnp.concatenate([dense_lo[c, rows, :] for c in couples], axis=1)
             low = jnp.dot(left, right[:, :QUERIES], preferred_element_type=F32)
             total = both[:, :QUERIES] + both[:, QUERIES:] + low
-            part[pl.ds(at, 8)] = part[pl.ds(at, 8)] + total.reshape(8, BLOCK, QUERIES)
+            part[pl.ds(at, size)] = part[pl.ds(at, size)] + total.reshape(size, BLOCK, QUERIES)
 
     def half_rows(u):
         return pl.ds(u * TILE, TILE)
@@ -251,11 +251,10 @@
 
     for h in range(HOPS):
 
-        def crossing(o):
-            block = (z + o) % NZ
+        def crossing(block):
             return remote(
                 part.at[other * 8 + block], cross.at[h, block],
-                sent_sem.at[0, h], cross_sem.at[h, o], (p, z * 2 + other),
+                sent_sem.at[0, h], cross_sem.at[h, block], (p, z * 2 + other),
             )
 
         order = (4, 3, 5, 1, 7, 2, 6, 0)
@@ -272,13 +271,15 @@
                 multiply(n + n // 2, 0, 2)
 
             columns(2)
-            multiply(2, other * 8, 1)
-            for o in order:
-                crossing(o).start()
+            for n in (1, 0):
+                four = (z // 4 + n) % 2 * 4
+                multiply(2, other * 8 + four, 1, 4)
+                for k in range(4):
+                    crossing(four + (z + k) % 4).start()
             multiply(2, core * 8, 1)
         else:
             for o in order:
-                crossing(o).start()
+                crossing((z + o) % NZ).start()
 
         def sum_of(o):
             return cross.at[h, (z + o) % NZ]
@@ -293,8 +294,8 @@
             along(way, n, u, ring.at[h, way, n, half_rows(u)], 1).wait_recv()
 
         for o in order:
-            crossing(o).wait_recv()
             block = (z + o) % NZ
+            crossing(block).wait_recv()
             cross[h, block] = cross[h, block] + part[core * 8 + block]
             if o == 4:
                 along(0, 3, 0, sum_of(4).at[half_rows(0)], 2).start()

time: 92 us -> 91.3 us (level)
    pallas_call x1, Pallas kernels: 80.1 us -> 78.9 us  [run_chain(): pl.pallas_call(chain_kernel, out_shape=jax.ShapeDtypeStruct((BLOCK, QUERI...]
where the time goes in v6:
time: 91.3 us; the launch traced here: 91.4 us
  Pallas kernels  90 us (99%)
  local copies, waits for them, and re-layouts  1.47 us (2%)
    pallas_call x1, Pallas kernels, run_chain(): pl.pallas_call(chain_kernel, out_shape=jax.ShapeDtypeStruct((BLOCK, QUERI...  78.9 us
    pallas_call x1, Pallas kernels, merge(): pl.pallas_call(merge_kernel, out_shape=(jax.ShapeDtypeStruct((HOPS - 1, S...  11.1 us

profile of v6, /device:TPU:1, one launch (start us, length us, event | category | flops | bytes accessed | tf_op | source)
XLA Modules:
  0.0 91.4 jit_solution(11525778770779306725)
XLA Ops:
  0.0 11.1 %first_hop_and_cells.1 = (f32[2,257,64,128]{3,2,1,0:T(8,128)}, s32[24,128]{1,0:T(8,128)}, f32[32,64,128]{2,1,0:T(8,128)}) custom-call(s32[3]{0:T(128)} %chain_hbm.1, s32[3]{0:T(128)} %bitcast.8, s32[3,2,256]{2,1,0:T(2,128)} %bitcast.7, s32[1,128]{1,0:T(1,128)} %bitcast.9, f32[3,128,64,128]{3,2,1,0:T(8,128)} %bitcast.5), custom_call_target="tpu_custom_call" | custom-call | tf_op jit(solution)/shard_map/first_hop_and_cells/pallas_call | solution.py:125
  11.1 78.9 %relation_chain.1 = f32[128,128]{1,0:T(8,128)} custom-call(s32[24,128]{1,0:T(8,128)} %get-tuple-element.8.table_hbm, f32[16,128,128]{2,1,0:T(8,128)} %bitcast.6, f32[2,257,64,128]{3,2,1,0:T(8,128)} %get-tuple-element.10.cells), custom_call_target="tpu_custom_call" | custom-call | tf_op jit(solution)/shard_map/relation_chain/pallas_call | solution.py:377
  90.0 1.5 %copy.7 = f32[128,128]{1,0:T(8,128)} copy(f32[128,128]{1,0:T(8,128)} %relation_chain.1) | data formatting | bytes 131072

commit v7 on v6

--- a/solution.py
+++ b/solution.py
@@ -341,11 +341,10 @@
                     spread(u, p, across(u, d), first_sem.at[h, u, NX - d - 1])
                 for e in (1, 3, 2):
                     spread(u, p, across(1 - u, e), group_sem.at[h, 0])
-            for d in (1, 3, 2):
-                for u in range(2):
-                    arrived(h, u, d)
-                    for e in (1, 3, 2):
-                        spread(u, across(u, d), across(1 - u, e), group_sem.at[h, d])
+            for u, d in ((0, 1), (0, 3), (1, 1), (0, 2), (1, 3), (1, 2)):
+                arrived(h, u, d)
+                for e in (1, 3, 2):
+                    spread(u, across(u, d), across(1 - u, e), group_sem.at[h, d])
         else:
             for u in range(2):
                 out[half_rows(u), :] = finished(u)

time: 91.3 us -> 93.1 us (1.020)
  Pallas kernels: 90 us -> 92.6 us
    pallas_call x1, Pallas kernels: 78.9 us -> 82.3 us  [run_chain(): pl.pallas_call(chain_kernel, out_shape=jax.ShapeDtypeStruct((BLOCK, QUERI...]
where the time goes in v7:
time: 93.1 us; the launch traced here: 94.1 us
  Pallas kernels  92.6 us (99%)
  local copies, waits for them, and re-layouts  1.47 us (2%)
    pallas_call x1, Pallas kernels, run_chain(): pl.pallas_call(chain_kernel, out_shape=jax.ShapeDtypeStruct((BLOCK, QUERI...  82.3 us
    pallas_call x1, Pallas kernels, merge(): pl.pallas_call(merge_kernel, out_shape=(jax.ShapeDtypeStruct((HOPS - 1, S...  10.3 us

profile of v7, /device:TPU:1, one launch (start us, length us, event | category | flops | bytes accessed | tf_op | source)
XLA Modules:
  0.0 94.1 jit_solution(13144681154026526668)
XLA Ops:
  0.0 10.3 %first_hop_and_cells.1 = (f32[2,257,64,128]{3,2,1,0:T(8,128)}, s32[24,128]{1,0:T(8,128)}, f32[32,64,128]{2,1,0:T(8,128)}) custom-call(s32[3]{0:T(128)} %chain_hbm.1, s32[3]{0:T(128)} %bitcast.8, s32[3,2,256]{2,1,0:T(2,128)} %bitcast.7, s32[1,128]{1,0:T(1,128)} %bitcast.9, f32[3,128,64,128]{3,2,1,0:T(8,128)} %bitcast.5), custom_call_target="tpu_custom_call" | custom-call | tf_op jit(solution)/shard_map/first_hop_and_cells/pallas_call | solution.py:125
  10.3 82.3 %relation_chain.1 = f32[128,128]{1,0:T(8,128)} custom-call(s32[24,128]{1,0:T(8,128)} %get-tuple-element.8.table_hbm, f32[16,128,128]{2,1,0:T(8,128)} %bitcast.6, f32[2,257,64,128]{3,2,1,0:T(8,128)} %get-tuple-element.10.cells), custom_call_target="tpu_custom_call" | custom-call | tf_op jit(solution)/shard_map/relation_chain/pallas_call | solution.py:376
  92.6 1.5 %copy.7 = f32[128,128]{1,0:T(8,128)} copy(f32[128,128]{1,0:T(8,128)} %relation_chain.1) | data formatting | bytes 131072
